TPU v7x, 128 devices: a whole 4x4x4 slice. The times are simulated.
128 devices in a mesh: mem: 4 (over z), var: 32 (over y, x, core).
Axes of the slice: x: 4, y: 4, z: 4, core: 2. Of those that a mesh axis runs over, the one named last changes fastest.
Arguments:
- prior_state: float32 [256, 262144], P(('mem', 'var')), may hold values from -6 to 6
- obs_value: float32 [2, 1024], replicated, may hold values from -6 to 6
- obs_error: float32 [2, 1024], replicated, may hold values from 0.5 to 2
- obs_owner: int32 [2, 1024], replicated, may hold values from 0 to 127, as said below
- obs_offset: int32 [2, 1024], replicated, may hold values from 0 to 2047
- taper_table: float32 [64], replicated, may hold values from 0 to 1.3, as said below
Outputs:
- posterior_state: float32 [256, 262144], P(('mem', 'var'))
Inputs may be any that keep to these rules, and one draw needn't show every extreme that they name: `taper_table`: the weights follow the Gaspari-Cohn shape over the bins, each bin scaled by its own factor; the last bin is zero. `obs_owner`: in each block every owner holds exactly 8 observations.
All inputs are finite; a program needn't handle non-finite values.
Results may differ from a plain program's by a relative error of at most 0.0003.
Values sent between devices are 32-bit elements; how exact they have to be, the bound alone decides.
No kernel may reach another device: no remote copies, remote signals or barrier semaphores. Data moves between devices by JAX's collectives and lax.ppermute only.
A program may use at most 64 MiB of HBM per device.

v0:
```python
import jax
import jax.numpy as jnp
from jax import lax
from jax.sharding import PartitionSpec as P

MEMBERS = 256
BLOCKS = 2
NBINS = 64


def increments(prior, value, error):
    mean = jnp.mean(prior, axis=1, keepdims=True)
    anom = prior - mean
    varian = jnp.sum(anom * anom, axis=1) / (MEMBERS - 1) + 1e-06
    noise = error[:, None]
    spread = varian[:, None]
    post_mean = (noise * mean + spread * value[:, None]) / (spread + noise)
    shrink = jnp.sqrt(noise / (spread + noise))
    return (anom, varian, post_mean + shrink * anom - prior)


def update_block(states, start, anom, varian, change, obs_pos, taper_table, bin_width):
    width = states.shape[1]
    centred = states - jnp.mean(states, axis=0, keepdims=True)
    cov = jnp.dot(
        anom, centred, precision=lax.Precision.HIGHEST, preferred_element_type=jnp.float32
    ) / (MEMBERS - 1)
    places = start + jnp.arange(width, dtype=jnp.int32)
    dist = jnp.abs(places[None, :] - obs_pos[:, None])
    bins = jnp.minimum(dist // bin_width, NBINS - 1)
    gain = jnp.take(taper_table, bins) * cov / varian[:, None]
    return states + jnp.dot(
        change.T, gain, precision=lax.Precision.HIGHEST, preferred_element_type=jnp.float32
    )


def body(prior_state, obs_value, obs_error, obs_owner, obs_offset, taper_table):
    n_mem = lax.axis_size("mem")
    n_var = lax.axis_size("var")
    n_dev = n_mem * n_var
    per_dev = prior_state.shape[0]
    total = per_dev * n_dev
    local_vars = prior_state.shape[1] // n_dev
    bin_width = prior_state.shape[1] // NBINS
    state = lax.all_to_all(prior_state, ("mem", "var"), split_axis=1, concat_axis=0, tiled=True)
    self_id = lax.axis_index(("mem", "var"))
    base = self_id * local_vars
    count = max(1, local_vars // 2048)
    size_blk = local_vars // count
    starts = base + jnp.arange(count, dtype=jnp.int32) * size_blk
    for block in range(BLOCKS):
        owner = obs_owner[block]
        offset = obs_offset[block]
        obs_pos = owner * local_vars + offset
        mine = (owner == self_id)[:, None]
        local = jnp.where(mine, jnp.take(state, offset, axis=1).T, 0.0)
        anom_own, varian_own, change_own = increments(local, obs_value[block], obs_error[block])
        anom, change = lax.psum(
            (jnp.where(mine, anom_own, 0.0), jnp.where(mine, change_own, 0.0)), ("mem", "var")
        )
        varian = jnp.sum(anom * anom, axis=1) / (MEMBERS - 1) + 1e-06
        pieces = state.reshape(total, count, size_blk).transpose(1, 0, 2)

        def one(item):
            return update_block(
                item[0], item[1], anom, varian, change, obs_pos, taper_table, bin_width
            )

        pieces = lax.map(one, (pieces, starts))
        state = pieces.transpose(1, 0, 2).reshape(total, local_vars)
    return lax.all_to_all(state, ("mem", "var"), split_axis=0, concat_axis=1, tiled=True)


def solution(mesh):
    in_specs = (P(("mem", "var"), None), P(), P(), P(), P(), P())
    out_specs = P(("mem", "var"), None)
    return jax.shard_map(body, mesh=mesh, in_specs=in_specs, out_specs=out_specs, check_vma=False)
```

profile of v0, /device:TPU:1, one launch (start us, length us, event | category | flops | bytes accessed | tf_op | source)
XLA Modules:
  0.0 623.4 jit_solution(16434754259857481911)
XLA Ops:
  6.5 11.5 %all-to-all-start = ((f32[2,128,2048]{2,0,1:T(2,128)}), f32[2,128,2048]{2,0,1:T(2,128)S(1)}, u32[]{:S(2)}, u32[]{:S(2)}) async-start(f32[2,128,2048]{2,0,1:T(2,128)} %bitcast.191), calls=%async_computation | async-start | bytes 4194304 | tf_op jit(solution)/shard_map/all_to_all | solution.py:45
  18.1 1.6 fusion.452
  19.7 0.8 compare_reduce_fusion
  20.5 0.8 fusion.446
  21.3 0.8 slice_multiply_fusion
  22.1 0.8 fusion.444
  22.9 0.8 fusion.445
  23.7 24.9 %all-to-all-done = f32[2,128,2048]{2,0,1:T(2,128)S(1)} async-done(((f32[2,128,2048]{2,0,1:T(2,128)}), f32[2,128,2048]{2,0,1:T(2,128)S(1)}, u32[]{:S(2)}, u32[]{:S(2)}) %all-to-all-start) | async-done | bytes 2097184 | tf_op jit(solution)/shard_map/all_to_all | solution.py:45
  48.6 1.3 copy-done.1
  49.9 2.4 squeeze.20
  52.3 1.9 copy.8
  54.3 3.5 gather_fusion
  58.3 1.8 fusion.300
  60.1 2.4 fusion.297
  63.0 0.7 fusion.450
  63.7 0.7 fusion.449
  65.2 2.3 reduce_sum.76
  67.5 141.2 %all-reduce.7.cloned.1.call-done = (f32[1024,256]{1,0:T(8,128)}, f32[1024,256]{1,0:T(8,128)}) async-done(((f32[1024,256]{1,0:T(8,128)}, f32[1024,256]{1,0:T(8,128)}), (f32[1024,256]{1,0:T(8,128)}, f32[1024,256]{1,0:T(8,128)})) %all-reduce.7.cloned.1.call-update) | async-done | bytes 2097168 | tf_op jit(solution)/shard_map/psum | solution.py:58
  208.7 1.4 multiply_reduce_fusion.2
  210.2 8.8 %fusion.294 = f32[1024,2048]{1,0:T(8,128)S(1)} fusion(f32[1024,256]{1,0:T(8,128)} %get-tuple-element.55, f32[256,2048]{1,0:T(8,128)S(1)} %copy-done, f32[2048]{0:T(1024)S(1)} %broadcast_multiply_fusion.1), kind=kOutput, calls=%fused_computation.306 | convolution fusion | flops 6442975232 | bytes 11542528 | tf_op jit(solution)/shard_map/while/body/eval_jaxpr/dot_general | solution.py:25
  218.9 93.7 %fusion.453 = (f32[2048]{0:T(1024)S(1)}, f32[256,2048]{1,0:T(8,128)}) fusion(f32[256,2048]{1,0:T(8,128)S(1)} %copy-done, f32[1024,256]{1,0:T(8,128)S(1)} %copy-done.4, f32[1024,2048]{1,0:T(8,128)S(1)} %fusion.294, f32[]{:T(128)} %bitcast.71, f32[]{:T(128)} %bitcast.70, f32[]{:T(128)} %bitcast.69, f32[]{:T(128)} %bitcast.68, f32[]{:T(128)} %bitcast.67, ...), kind=kOutput, calls=%fused_computation.496 | convolution fusion | flops 6766458880 | bytes 13656320 | tf_op jit(solution)/shard_map/while/body/eval_jaxpr/dot_general | solution.py:32
  312.7 1.9 copy.9
  314.6 3.5 gather_fusion.1
  318.6 1.8 fusion.301
  320.4 2.3 fusion.296
  322.8 149.2 %all-reduce.5.cloned.1.call-done = (f32[1024,256]{1,0:T(8,128)}, f32[1024,256]{1,0:T(8,128)}) async-done(((f32[1024,256]{1,0:T(8,128)}, f32[1024,256]{1,0:T(8,128)}), (f32[1024,256]{1,0:T(8,128)}, f32[1024,256]{1,0:T(8,128)})) %all-reduce.5.cloned.1.call-update) | async-done | bytes 2097168 | tf_op jit(solution)/shard_map/psum | solution.py:58
  471.9 1.4 multiply_reduce_fusion
  473.4 8.8 %fusion.292 = f32[1024,2048]{1,0:T(8,128)S(1)} fusion(f32[1024,256]{1,0:T(8,128)} %get-tuple-element.44, f32[256,2048]{1,0:T(8,128)S(1)} %copy-done.2, f32[2048]{0:T(1024)S(1)} %broadcast_multiply_fusion), kind=kOutput, calls=%fused_computation.304 | convolution fusion | flops 6442975232 | bytes 11542528 | tf_op jit(solution)/shard_map/while/body/eval_jaxpr/dot_general | solution.py:25
  482.2 93.3 %fusion.289 = f32[256,2048]{1,0:T(8,128)} fusion(f32[256,2048]{1,0:T(8,128)S(1)} %copy-done.2, f32[1024,256]{1,0:T(8,128)S(1)} %copy-done.5, f32[1024,2048]{1,0:T(8,128)S(1)} %fusion.292, f32[]{:T(128)} %bitcast.71, f32[]{:T(128)} %bitcast.70, f32[]{:T(128)} %bitcast.69, f32[]{:T(128)} %bitcast.68, f32[]{:T(128)} %bitcast.67, f32[]{:T(128)} %bitcast.66, ...), kind=kOutput, calls=%fused_computation.303 | convolution fusion | flops 6765936640 | bytes 13648128 | tf_op jit(solution)/shard_map/while/body/eval_jaxpr/dot_general | solution.py:32
  575.5 2.5 all_to_all.29
  578.0 37.0 %all_to_all.35 = f32[128,2,2048]{2,1,0:T(2,128)S(1)} all-to-all(f32[128,2,2048]{2,1,0:T(2,128)S(1)} %all_to_all.29), channel_id=1, replica_groups=mesh['mem'=4,'var'=32] {'mem','var'}, dimensions={0} | all-to-all | bytes 4194304 | tf_op jit(solution)/shard_map/all_to_all | solution.py:71
  615.0 1.3 copy.16
  (31 shorter events, 2.4 us)
Async XLA Ops:
  6.5 42.0 %all-to-all-start = ((f32[2,128,2048]{2,0,1:T(2,128)}), f32[2,128,2048]{2,0,1:T(2,128)S(1)}, u32[]{:S(2)}, u32[]{:S(2)}) async-start(f32[2,128,2048]{2,0,1:T(2,128)} %bitcast.191), calls=%async_computation | async-start | bytes 4194304 | tf_op jit(solution)/shard_map/all_to_all | solution.py:45
  18.0 190.6 %all-reduce.7.cloned.1.call-start = ((), (), s32[]{:S(2)}) async-start(), calls=%async_computation.3 | async-start | bytes 4194304 | tf_op jit(solution)/shard_map/psum | solution.py:58
  48.6 1.4 copy-start.1
  54.3 8.7 %copy-start.3 = (f32[64]{0:T(128)S(1)}, f32[64]{0:T(128)}, u32[]{:S(2)}) copy-start(f32[64]{0:T(128)} %param.15) | copy-start | bytes 772
  57.7 152.4 %copy-start = (f32[256,2048]{1,0:T(8,128)S(1)}, f32[256,2048]{1,0:T(8,128)}, u32[]{:S(2)}) copy-start(f32[256,2048]{1,0:T(8,128)} %squeeze.20) | copy-start | bytes 6291460
  62.4 409.5 %all-reduce.5.cloned.1.call-start = ((), (), s32[]{:S(2)}) async-start(), calls=%async_computation.2 | async-start | bytes 4194304 | tf_op jit(solution)/shard_map/psum | solution.py:58
  210.1 8.8 %copy-start.4 = (f32[1024,256]{1,0:T(8,128)S(1)}, f32[1024,256]{1,0:T(8,128)}, u32[]{:S(2)}) copy-start(f32[1024,256]{1,0:T(8,128)} %get-tuple-element.54) | copy-start | bytes 3145732
  318.1 155.3 %copy-start.2 = (f32[256,2048]{1,0:T(8,128)S(1)}, f32[256,2048]{1,0:T(8,128)}, u32[]{:S(2)}) copy-start(f32[256,2048]{1,0:T(8,128)} %get-tuple-element.152) | copy-start | bytes 6291460
  473.4 8.8 %copy-start.5 = (f32[1024,256]{1,0:T(8,128)S(1)}, f32[1024,256]{1,0:T(8,128)}, u32[]{:S(2)}) copy-start(f32[1024,256]{1,0:T(8,128)} %get-tuple-element.43) | copy-start | bytes 3145732
Sparse Core Ops, SparseCore 0:
  62.6 146.0 all-reduce.6
  322.9 149.0 all-reduce.4
where the time goes:
time: 628 us; the launch traced here: 623 us
  waiting for transfers between devices  315 us (50%)
  matrix products  205 us (33%)
  blocking collectives  37 us (6%)
  local copies, waits for them, and re-layouts  24.5 us (4%)
  other arithmetic  16.1 us (3%)
  between operations  13.9 us (2%)
  starting transfers between devices  12 us (2%)
    psum x2, waiting for transfers between devices, body(): lax.psum((jnp.where(mine, anom_own, 0.0), jnp.where(mine, change_own, 0.0...  290 us
    dot_general x2, matrix products, update_block(): jnp.dot(change.T, gain, precision=lax.Precision.HIGHEST, preferred_elemen...  187 us
    all_to_all x1, blocking collectives, body(): lax.all_to_all(state, ('mem', 'var'), split_axis=0, concat_axis=1, tiled=...  37 us
    all_to_all x1, waiting for transfers between devices, body(): lax.all_to_all(prior_state, ('mem', 'var'), split_axis=1, concat_axis=0,...  24.9 us
    dot_general x2, matrix products, update_block(): jnp.dot(anom, centred, precision=lax.Precision.HIGHEST, preferred_element...  17.5 us
  transfers between devices with their start and end apart: 3, of which 3 were waited for; matrix products, arithmetic and copies ran while one was open for 2% of the time, Pallas kernels for 0%

commit v1 on v0

v1 whole, which is shorter than its diff:
```python
import functools

import jax
import jax.numpy as jnp
from jax import lax
from jax.experimental import pallas as pl
from jax.experimental.layout import Layout, with_layout_constraint
from jax.experimental.pallas import tpu as pltpu
from jax.sharding import PartitionSpec as P

MEMBERS = 256
NDEV = 128
NOBS = 1024
HALF = NOBS // 2
NV_DEV = 2048
LANES = 128
TILES = NV_DEV // LANES
STATE_ROWS = 2 * TILES
OBS_ROWS = 32
MSG = STATE_ROWS + OBS_ROWS
WIDE = 256
F32 = jnp.float32
BF16 = jnp.bfloat16


def iota(shape, dim):
    return lax.broadcasted_iota(jnp.int32, shape, dim)


def split(x):
    hi = x.astype(BF16)
    return hi, (x - hi.astype(F32)).astype(BF16)


def dot3(a, b, dims=(((1,), (0,)), ((), ()))):
    ca, cb = dims[0][0][0], dims[0][1][0]
    left = jnp.concatenate([a[0], a[1], a[0]], axis=ca)
    right = jnp.concatenate([b[0], b[0], b[1]], axis=cb)
    return lax.dot_general(left, right, dims, preferred_element_type=F32)


def by_parity(x):
    lane = iota((4, LANES), 1)
    first, second = x[0:4], x[4:8]
    even = jnp.where(lane < 64, first, pltpu.roll(second, 64, 1))
    odd = jnp.where(lane < 64, pltpu.roll(first, 64, 1), second)
    return even, odd


def prep_kernel(me_ref, owner_ref, offset_ref, value_ref, error_ref, state_ref, msg_ref, field_ref):
    odd_device = me_ref[0] % 2 == 1
    row = iota((LANES, LANES), 0)
    row_owner = (2 * row) % LANES + row // 64
    before = jnp.where(row < iota((LANES, LANES), 1), 1.0, 0.0).astype(BF16)
    slot = iota((8, NOBS), 0).astype(F32)
    tables = []
    for b in range(2):
        hot = []
        ranks = []
        count = jnp.zeros((LANES, 1), F32)
        for t in range(NOBS // LANES):
            own = owner_ref[b : b + 1, t * LANES : (t + 1) * LANES]
            is_own = jnp.where(own == row_owner, 1.0, 0.0)
            ahead = jnp.dot(is_own.astype(BF16), before, preferred_element_type=F32) + count
            ranks.append(jnp.sum(is_own * ahead, axis=0, keepdims=True))
            count = count + jnp.sum(is_own, axis=1, keepdims=True)
            hot.append(is_own.astype(BF16))
        hot = jnp.concatenate(hot, axis=1)
        here = jnp.concatenate(ranks, axis=1) == slot
        off = offset_ref[b : b + 1, :]
        parts = [(off // LANES).astype(F32), (off % LANES).astype(F32)]
        for ref in (value_ref, error_ref):
            rest = ref[b : b + 1, :]
            for _ in range(3):
                part = rest.astype(BF16).astype(F32)
                parts.append(part)
                rest = rest - part
        rows = jnp.concatenate([jnp.where(here, p, 0.0).astype(BF16) for p in parts], axis=0)
        tables.append(
            lax.dot_general(rows, hot, (((1,), (1,)), ((), ())), preferred_element_type=F32)
        )
    for b in range(2):
        t = tables[b]
        off = t[0:8] * float(LANES) + t[8:16]
        val = (t[16:24] + t[24:32]) + t[32:40]
        err = (t[40:48] + t[48:56]) + t[56:64]
        for f, x in enumerate((off, val, err)):
            even, odd = by_parity(x)
            same = jnp.where(odd_device, odd, even)
            other = jnp.where(odd_device, even, odd)
            field_ref[(b * 3 + f) * 8 : (b * 3 + f) * 8 + 8, :] = jnp.concatenate([same, other], axis=0)
    pad = jnp.zeros((LANES - 16, LANES), F32)
    tile_of = jnp.concatenate([tables[0][0:8], tables[1][0:8], pad], axis=0).T.astype(jnp.int32)
    lane_of = jnp.concatenate([tables[0][8:16], tables[1][8:16], pad], axis=0).T.astype(jnp.int32)
    picked = []
    for r in range(2):
        groups = []
        for g in range(16):
            want_tile = tile_of[g * 8 : g * 8 + 8, :]
            want_lane = lane_of[g * 8 : g * 8 + 8, :]
            first = 16 * g if g < 8 else 16 * (g - 8) + 1
            acc = jnp.zeros((8, LANES), F32)
            for c in range(TILES):
                x = state_ref[pl.ds(first * STATE_ROWS + c * 2 + r, 8, stride=2 * STATE_ROWS), :]
                acc = jnp.where(want_tile == c, jnp.take_along_axis(x, want_lane, axis=1), acc)
            groups.append(acc)
        found = jnp.concatenate(groups, axis=0).T
        for b in range(2):
            even, odd = by_parity(found[b * 8 : b * 8 + 8])
            picked.extend([even, odd])
    picked = jnp.concatenate(picked, axis=0)

    def fill(d, _):
        msg_ref[pl.ds(d * MSG, STATE_ROWS), :] = state_ref[pl.ds(d * STATE_ROWS, STATE_ROWS), :]
        msg_ref[pl.ds(d * MSG + STATE_ROWS, OBS_ROWS), :] = picked
        return 0

    lax.fori_loop(0, NDEV, fill, 0, unroll=8)


def columns(row):
    return jnp.broadcast_to(row, (LANES, LANES)).T


def stats(raw, value, error):
    mean = jnp.sum(raw, axis=0, keepdims=True) * (1.0 / MEMBERS)
    anom = raw - mean
    varian = jnp.sum(anom * anom, axis=0, keepdims=True) * (1.0 / (MEMBERS - 1)) + 1e-06
    total = varian + error
    shrink = jnp.sqrt(error / total)
    scale = -1.0 / ((MEMBERS - 1) * total * (1.0 + shrink))
    push = anom - (value - mean) * (1.0 + shrink)
    return anom, anom * scale, push


def main_kernel(
    me_ref, table_ref, field_ref, recv_ref, out_ref,
    left_hi, left_lo, push_hi, push_lo, const_hi, const_lo, thr, low, high, off_col, raw2,
):
    me = me_ref[0]
    par = me % 2
    mine = me // 2
    table8 = jnp.broadcast_to(table_ref[...], (8, LANES))
    table = jnp.broadcast_to(table_ref[...], (LANES, LANES))

    def load_obs(b):
        out = []
        for which in (par, 1 - par):
            for s in range(4):
                at = STATE_ROWS + b * 8 + which * 4 + s
                out.append(
                    jnp.concatenate(
                        [recv_ref[pl.ds(at + r * 16, NDEV, stride=MSG), :] for r in range(2)], axis=0
                    )
                )
        return jnp.concatenate(out, axis=1)

    def field(b, f):
        base = (b * 3 + f) * 8
        return jnp.concatenate([field_ref[base + i : base + i + 1, :] for i in range(8)], axis=1)

    lane64 = iota((8, LANES), 1) % 64
    delta = mine - lane64
    steps = jnp.abs(delta)
    w_far = jnp.take_along_axis(table8, steps, axis=1)[0:1]
    w_near = jnp.take_along_axis(table8, jnp.maximum(steps - 1, 0), axis=1)[0:1]
    w_other = jnp.take_along_axis(table8, jnp.abs(2 * delta + 2 * par - 1) // 2, axis=1)[0:1]
    ahead = delta[0:1] > 0
    w_low = jnp.where(ahead, w_near, w_far)
    w_high = jnp.where(ahead, w_far, w_near)
    shift = jnp.where(ahead, 0.0, 1.0)
    w_other4 = jnp.concatenate([w_other] * 4, axis=1)

    def block_setup(b, raw):
        anom, scaled, push = stats(raw, field(b, 1), field(b, 2))
        hi, lo = split(scaled.T)
        left_hi[b, :, :] = hi
        left_lo[b, :, :] = lo
        ph, pw = split(push)
        push_hi[b, :, :] = ph
        push_lo[b, :, :] = pw
        weighted = split(scaled[:, HALF:] * w_other4)
        const = dot3((ph[:, HALF:], pw[:, HALF:]), weighted, (((1,), (1,)), ((), ())))
        ch, cl = split(const)
        const_hi[b, :, :] = ch
        const_lo[b, :, :] = cl
        off = field(b, 0)
        for s in range(4):
            thr[b, s * LANES : (s + 1) * LANES, :] = columns(off[:, s * LANES : (s + 1) * LANES] + shift)
        return off

    low[...] = columns(w_low)
    high[...] = columns(w_high)

    off1 = block_setup(0, load_obs(0))
    for s in range(8):
        off_col[s * LANES : (s + 1) * LANES, :] = columns(off1[:, s * LANES : (s + 1) * LANES])
    raw2[...] = load_obs(1)

    d = iota((LANES, LANES), 1) % 64 - iota((LANES, LANES), 0) % 64
    ad = jnp.abs(d)
    far = jnp.take_along_axis(table, ad, axis=1)
    near = jnp.take_along_axis(table, jnp.maximum(ad - 1, 0), axis=1)
    sign = jnp.where(d > 0, 1.0, jnp.where(d < 0, -1.0, 0.0))
    to_same = jnp.take_along_axis(table, jnp.abs(2 * d + 2 * par - 1) // 2, axis=1)
    to_other = jnp.take_along_axis(table, jnp.abs(2 * d + 1 - 2 * par) // 2, axis=1)
    off2 = field(1, 0)
    for t in range(NOBS // WIDE):
        raw = raw2[:, t * WIDE : (t + 1) * WIDE]
        centred = raw - jnp.sum(raw, axis=0, keepdims=True) * (1.0 / MEMBERS)
        cov = dot3((left_hi[0], left_lo[0]), split(centred))
        in_same = t < NOBS // WIDE // 2
        pieces = []
        for k in range(8):
            line = []
            for h in range(WIDE // LANES):
                c = cov[k * LANES : (k + 1) * LANES, h * LANES : (h + 1) * LANES]
                if (k < 4) == in_same:
                    at = t * WIDE + h * LANES
                    gap = off2[:, at : at + LANES] - off_col[k * LANES : (k + 1) * LANES, :]
                    w = jnp.where(gap * sign >= 0.0, far, near)
                else:
                    w = to_same if in_same else to_other
                line.append(c * w)
            pieces.append(jnp.concatenate(line, axis=1))
        gain = split(jnp.concatenate(pieces, axis=0))
        raw2[:, t * WIDE : (t + 1) * WIDE] = raw + dot3((push_hi[0], push_lo[0]), gain)
    block_setup(1, raw2[...])

    def tile(t, _):
        at = t * (WIDE // LANES)
        raw = jnp.concatenate(
            [
                jnp.concatenate(
                    [recv_ref[pl.ds((at + h) * 2 + r, NDEV, stride=MSG), :] for r in range(2)], axis=0
                )
                for h in range(WIDE // LANES)
            ],
            axis=1,
        )
        place = [(iota((LANES, LANES), 1) + (at + h) * LANES).astype(F32) for h in range(WIDE // LANES)]
        for b in range(2):
            centred = split(raw - jnp.sum(raw, axis=0, keepdims=True) * (1.0 / MEMBERS))
            cov = dot3((left_hi[b, 0:HALF, :], left_lo[b, 0:HALF, :]), centred)
            pieces = []
            for k in range(4):
                line = []
                for h in range(WIDE // LANES):
                    c = cov[k * LANES : (k + 1) * LANES, h * LANES : (h + 1) * LANES]
                    w = jnp.where(place[h] >= thr[b, k * LANES : (k + 1) * LANES, :], high[...], low[...])
                    line.append(c * w)
                pieces.append(jnp.concatenate(line, axis=1))
            gain = split(jnp.concatenate(pieces, axis=0))
            left = (
                jnp.concatenate([push_hi[b, :, 0:HALF], const_hi[b]], axis=1),
                jnp.concatenate([push_lo[b, :, 0:HALF], const_lo[b]], axis=1),
            )
            right = tuple(jnp.concatenate([g, c], axis=0) for g, c in zip(gain, centred))
            raw = raw + dot3(left, right)
        for h in range(WIDE // LANES):
            for r in range(2):
                out_ref[pl.ds((at + h) * 2 + r, NDEV, stride=STATE_ROWS), :] = raw[
                    r * NDEV : (r + 1) * NDEV, h * LANES : (h + 1) * LANES
                ]
        return 0

    lax.fori_loop(0, NV_DEV // WIDE, tile, 0)


VMEM = pl.BlockSpec(memory_space=pltpu.VMEM)
SMEM = pl.BlockSpec(memory_space=pltpu.SMEM)
PARAMS = pltpu.CompilerParams(vmem_limit_bytes=48 * 1024 * 1024)


def prep(me, owner, offset, value, error, state):
    return pl.pallas_call(
        prep_kernel,
        out_shape=(
            jax.ShapeDtypeStruct((NDEV * MSG, LANES), F32),
            jax.ShapeDtypeStruct((48, LANES), F32),
        ),
        in_specs=[SMEM] + [VMEM] * 5,
        out_specs=(VMEM, VMEM),
        compiler_params=PARAMS,
        name="prep",
    )(me, owner, offset, value, error, state)


def assimilate(me, table, fields, recv):
    return pl.pallas_call(
        main_kernel,
        out_shape=jax.ShapeDtypeStruct((NDEV * STATE_ROWS, LANES), F32),
        in_specs=[SMEM] + [VMEM] * 3,
        out_specs=VMEM,
        scratch_shapes=[
            pltpu.VMEM((2, NOBS, MEMBERS), BF16),
            pltpu.VMEM((2, NOBS, MEMBERS), BF16),
            pltpu.VMEM((2, MEMBERS, NOBS), BF16),
            pltpu.VMEM((2, MEMBERS, NOBS), BF16),
            pltpu.VMEM((2, MEMBERS, MEMBERS), BF16),
            pltpu.VMEM((2, MEMBERS, MEMBERS), BF16),
            pltpu.VMEM((2, HALF, LANES), F32),
            pltpu.VMEM((LANES, LANES), F32),
            pltpu.VMEM((LANES, LANES), F32),
            pltpu.VMEM((NOBS, LANES), F32),
            pltpu.VMEM((MEMBERS, NOBS), F32),
        ],
        compiler_params=PARAMS,
        name="assimilate",
    )(me, table, fields, recv)


def body(prior_state, obs_value, obs_error, obs_owner, obs_offset, taper_table):
    axes = ("mem", "var")
    me = lax.axis_index(axes).astype(jnp.int32).reshape(1)
    table = jnp.pad(taper_table, (0, LANES - taper_table.shape[0])).reshape(1, LANES)
    rows = prior_state.reshape(2, NDEV * TILES, LANES).transpose(1, 0, 2).reshape(NDEV * STATE_ROWS, LANES)
    msg, fields = prep(me, obs_owner, obs_offset, obs_value, obs_error, rows)
    recv = lax.all_to_all(msg.reshape(NDEV, MSG, LANES), axes, split_axis=0, concat_axis=0, tiled=True)
    new = assimilate(me, table, fields, recv.reshape(NDEV * MSG, LANES))
    back = lax.all_to_all(
        new.reshape(NDEV, STATE_ROWS, LANES), axes, split_axis=0, concat_axis=0, tiled=True
    )
    rows = back.reshape(NDEV * TILES, 2, LANES).transpose(1, 0, 2)
    rows = with_layout_constraint(rows, Layout(major_to_minor=(1, 0, 2)))
    return rows.reshape(2, NDEV * NV_DEV)


def solution(mesh):
    in_specs = (P(("mem", "var"), None), P(), P(), P(), P(), P())
    out_specs = P(("mem", "var"), None)
    return jax.shard_map(body, mesh=mesh, in_specs=in_specs, out_specs=out_specs, check_vma=False)
```

time: 628 us -> 140 us (0.22)
  waiting for transfers between devices: 315 us -> 52.6 us
  matrix products: 205 us -> 0 us
  Pallas kernels: 0 us -> 35.1 us
  local copies, waits for them, and re-layouts: 24.5 us -> 5.7 us
  other arithmetic: 16.1 us -> 0 us
  between operations: 13.9 us -> 0.04 us
    psum x2 -> x0, waiting for transfers between devices: 290 us -> none  [body(): lax.psum((jnp.where(mine, anom_own, 0.0), jnp.where(mine, change_own, 0.0...]
    dot_general x4 -> x0, matrix products: 205 us -> none  [the longest x2 187 us: update_block(): jnp.dot(change.T, gain, precision=lax.Precision.HIGHEST, preferred_elemen...]
    pallas_call x0 -> x2, Pallas kernels: none -> 35.1 us  [the longest x1 30.7 us: assimilate(): pl.pallas_call(main_kernel, out_shape=jax.ShapeDtypeStruct((NDEV * STATE_...]
    all_to_all x1, waiting for transfers between devices: 24.9 us -> 52.6 us  [body(): lax.all_to_all(msg.reshape(NDEV, MSG, LANES), axes, split_axis=0, concat_...]
    gather x6 -> x0, local copies, waits for them, and re-layouts: 10.7 us -> none  [the longest x2 6.93 us: body(): local = jnp.where(mine, jnp.take(state, offset, axis=1).T, 0.0)]
    select_n x4 -> x0, other arithmetic: 8.26 us -> none  [the longest x2 4.7 us: body(): jnp.where(mine, change_own, 0.0)]
  transfers between devices with their start and end apart: 3 -> 1, of which waited for: 3 -> 1; matrix products, arithmetic and copies ran while one was open for 2% -> 0% of each run, Pallas kernels for 0% -> 0%
where the time goes in v1:
time: 140 us
  waiting for transfers between devices  52.6 us (38%)
  Pallas kernels  35.1 us (25%)
  blocking collectives  34.4 us (25%)
  starting transfers between devices  12 us (9%)
  local copies, waits for them, and re-layouts  5.7 us (4%)
    all_to_all x1, waiting for transfers between devices, body(): lax.all_to_all(msg.reshape(NDEV, MSG, LANES), axes, split_axis=0, concat_...  52.6 us
    all_to_all x1, blocking collectives, body(): lax.all_to_all(new.reshape(NDEV, STATE_ROWS, LANES), axes, split_axis=0,...  34.4 us
    pallas_call x1, Pallas kernels, assimilate(): pl.pallas_call(main_kernel, out_shape=jax.ShapeDtypeStruct((NDEV * STATE_...  30.7 us
    all_to_all x1, starting transfers between devices, body(): lax.all_to_all(msg.reshape(NDEV, MSG, LANES), axes, split_axis=0, concat_...  12 us
    unnamed x13, local copies, waits for them, and re-layouts  5.7 us
    pallas_call x1, Pallas kernels, prep(): pl.pallas_call(prep_kernel, out_shape=(jax.ShapeDtypeStruct((NDEV * MSG,...  4.39 us
  transfers between devices with their start and end apart: 1, of which 1 were waited for; matrix products, arithmetic and copies ran while one was open for 0% of the time, Pallas kernels for 0%

profile of v1, /device:TPU:1, one launch (start us, length us, event | category | flops | bytes accessed | tf_op | source)
XLA Modules:
  0.0 139.8 jit_solution(13749486069916332239)
XLA Ops:
  0.0 0.0 copy-start
  0.0 1.6 %copy-done = f32[2,262144]{1,0:T(2,128)S(1)} copy-done((f32[2,262144]{1,0:T(2,128)S(1)}, f32[2,262144]{1,0:T(2,128)}, u32[]{:S(2)}) %copy-start) | copy-done | bytes 2097176
  1.6 0.0 copy-start.1
  1.6 0.7 copy-done.1
  2.3 0.0 copy-start.2
  2.3 0.7 copy-done.2
  3.0 0.0 copy-start.3
  3.0 0.7 copy-done.3
  3.7 0.0 copy-start.4
  3.7 0.7 copy-done.4
  4.4 4.4 %prep.1 = (f32[8192,128]{1,0:T(8,128)}, f32[48,128]{1,0:T(8,128)S(1)}) custom-call(s32[1]{0:T(128)} %bitcast.me_ref, s32[2,1024]{1,0:T(2,128)S(1)} %copy-done.1, s32[2,1024]{1,0:T(2,128)S(1)} %copy-done.2, f32[2,1024]{1,0:T(2,128)S(1)} %copy-done.3, f32[2,1024]{1,0:T(2,128)S(1)} %copy-done.4, f32[4096,128]{1,0:T(8,128)S(1)} %bitcast.17), custom_call_target="tpu_custom_call" | custom-call | tf_op jit(solution)/shard_map/prep/pallas_call | solution.py:276
  8.8 0.0 copy-start.5
  8.8 12.0 %all-to-all-start = ((f32[128,64,128]{2,1,0:T(8,128)}), f32[128,64,128]{2,1,0:T(8,128)}, u32[]{:S(2)}, u32[]{:S(2)}) async-start(f32[128,64,128]{2,1,0:T(8,128)} %bitcast.19), calls=%async_computation | async-start | bytes 8388608 | tf_op jit(solution)/shard_map/all_to_all | solution.py:319
  20.7 0.0 copy-done.5
  20.8 52.6 %all-to-all-done = f32[128,64,128]{2,1,0:T(8,128)} async-done(((f32[128,64,128]{2,1,0:T(8,128)}), f32[128,64,128]{2,1,0:T(8,128)}, u32[]{:S(2)}, u32[]{:S(2)}) %all-to-all-start) | async-done | bytes 4194336 | tf_op jit(solution)/shard_map/all_to_all | solution.py:319
  73.4 30.7 %assimilate.1 = f32[4096,128]{1,0:T(8,128)S(1)} custom-call(s32[1]{0:T(128)} %bitcast.me_ref, f32[1,128]{1,0:T(1,128)S(1)} %pad_bitcast_fusion.table_ref, f32[48,128]{1,0:T(8,128)S(1)} %get-tuple-element.7.field_ref, f32[8192,128]{1,0:T(8,128)} %bitcast.6.recv_ref), custom_call_target="tpu_custom_call" | custom-call | tf_op jit(solution)/shard_map/assimilate/pallas_call | solution.py:290
  104.1 34.4 %all_to_all.10 = f32[128,32,128]{2,1,0:T(8,128)S(1)} all-to-all(f32[128,32,128]{2,1,0:T(8,128)S(1)} %bitcast.16), channel_id=1, replica_groups=mesh['mem'=4,'var'=32] {'mem','var'}, dimensions={0} | all-to-all | bytes 4194304 | tf_op jit(solution)/shard_map/all_to_all | solution.py:321
  138.5 1.3 copy.9
  (1 shorter events, 0.0 us)
Async XLA Ops:
  0.0 1.6 %copy-start = (f32[2,262144]{1,0:T(2,128)S(1)}, f32[2,262144]{1,0:T(2,128)}, u32[]{:S(2)}) copy-start(f32[2,262144]{1,0:T(2,128)} %param.6) | copy-start | bytes 6291460
  1.6 0.7 copy-start.1
  2.3 0.7 copy-start.2
  3.0 0.7 copy-start.3
  3.7 0.7 copy-start.4
  8.8 12.0 %copy-start.5 = (f32[64]{0:T(128)S(1)}, f32[64]{0:T(128)}, u32[]{:S(2)}) copy-start(f32[64]{0:T(128)} %param.11) | copy-start | bytes 772
  8.8 64.6 %all-to-all-start = ((f32[128,64,128]{2,1,0:T(8,128)}), f32[128,64,128]{2,1,0:T(8,128)}, u32[]{:S(2)}, u32[]{:S(2)}) async-start(f32[128,64,128]{2,1,0:T(8,128)} %bitcast.19), calls=%async_computation | async-start | bytes 8388608 | tf_op jit(solution)/shard_map/all_to_all | solution.py:319

commit v2 on v1

v2 whole, which is shorter than its diff:
```python
import functools

import jax
import jax.numpy as jnp
from jax import lax
from jax.experimental import pallas as pl
from jax.experimental.layout import Layout, with_layout_constraint
from jax.experimental.pallas import tpu as pltpu
from jax.sharding import PartitionSpec as P

MEMBERS = 256
NDEV = 128
NOBS = 1024
HALF = NOBS // 2
NV_DEV = 2048
LANES = 128
TILES = NV_DEV // LANES
STATE_ROWS = 2 * TILES
OBS_ROWS = 16
MSG = STATE_ROWS + OBS_ROWS
WIDE = 1024
OBS_WIDE = 512
F32 = jnp.float32
BF16 = jnp.bfloat16
VMEM_MIB = 32


def iota(shape, dim):
    return lax.broadcasted_iota(jnp.int32, shape, dim)


def split(x):
    hi = x.astype(BF16)
    return hi, (x - hi.astype(F32)).astype(BF16)


def dot3(a, b, dims=(((1,), (0,)), ((), ()))):
    ca, cb = dims[0][0][0], dims[0][1][0]
    left = jnp.concatenate([a[0], a[1], a[0]], axis=ca)
    right = jnp.concatenate([b[0], b[0], b[1]], axis=cb)
    return lax.dot_general(left, right, dims, preferred_element_type=F32)


def by_parity(x):
    lane = iota((4, LANES), 1)
    first, second = x[0:4], x[4:8]
    even = jnp.where(lane < 64, first, pltpu.roll(second, 64, 1))
    odd = jnp.where(lane < 64, pltpu.roll(first, 64, 1), second)
    return even, odd


def owner_of_row():
    row = iota((LANES, LANES), 0)
    return (2 * row) % LANES + row // 64


def prep_kernel(owner_hbm, offset_hbm, state_hbm, msg_ref, rank_ref, owner_ref, offset_ref, sems):
    rows_of = msg_ref.reshape(NDEV * MSG, LANES)
    state_copy = pltpu.make_async_copy(state_hbm, msg_ref.at[:, 0:STATE_ROWS, :], sems.at[0])
    owner_copy = pltpu.make_async_copy(owner_hbm, owner_ref, sems.at[1])
    offset_copy = pltpu.make_async_copy(offset_hbm, offset_ref, sems.at[2])
    owner_copy.start()
    offset_copy.start()
    state_copy.start()
    owner_copy.wait()
    offset_copy.wait()
    row_owner = owner_of_row()
    before = jnp.where(iota((LANES, LANES), 0) < iota((LANES, LANES), 1), 1.0, 0.0).astype(BF16)
    slot = iota((8, NOBS), 0).astype(F32)
    tables = []
    for b in range(2):
        hot = []
        ranks = []
        count = jnp.zeros((LANES, 1), F32)
        for t in range(NOBS // LANES):
            own = owner_ref[b : b + 1, t * LANES : (t + 1) * LANES]
            is_own = jnp.where(own == row_owner, 1.0, 0.0)
            ahead = jnp.dot(is_own.astype(BF16), before, preferred_element_type=F32) + count
            ranks.append(jnp.sum(is_own * ahead, axis=0, keepdims=True))
            count = count + jnp.sum(is_own, axis=1, keepdims=True)
            hot.append(is_own.astype(BF16))
        hot = jnp.concatenate(hot, axis=1)
        rank = jnp.concatenate(ranks, axis=1)
        rank_ref[b : b + 1, :] = rank
        here = rank == slot
        off = offset_ref[b : b + 1, :]
        parts = [(off // LANES).astype(F32), (off % LANES).astype(F32)]
        rows = jnp.concatenate([jnp.where(here, p, 0.0).astype(BF16) for p in parts], axis=0)
        tables.append(
            lax.dot_general(rows, hot, (((1,), (1,)), ((), ())), preferred_element_type=F32)
        )
    pad = jnp.zeros((LANES - 16, LANES), F32)
    tile_of = jnp.concatenate([tables[0][0:8], tables[1][0:8], pad], axis=0).T.astype(jnp.int32)
    lane_of = jnp.concatenate([tables[0][8:16], tables[1][8:16], pad], axis=0).T.astype(jnp.int32)
    state_copy.wait()
    even_rows = []
    odd_rows = []
    for r in range(2):
        groups = []
        for g in range(16):
            want_tile = tile_of[g * 8 : g * 8 + 8, :]
            want_lane = lane_of[g * 8 : g * 8 + 8, :]
            first = 16 * g if g < 8 else 16 * (g - 8) + 1
            acc = jnp.zeros((8, LANES), F32)
            for c in range(TILES):
                x = rows_of[pl.ds(first * MSG + c * 2 + r, 8, stride=2 * MSG), :]
                acc = jnp.where(want_tile == c, jnp.take_along_axis(x, want_lane, axis=1), acc)
            groups.append(acc)
        found = jnp.concatenate(groups, axis=0).T
        for b in range(2):
            even, odd = by_parity(found[b * 8 : b * 8 + 8])
            even_rows.append(even)
            odd_rows.append(odd)
    even_rows = jnp.concatenate(even_rows, axis=0)
    odd_rows = jnp.concatenate(odd_rows, axis=0)

    def fill(d, _):
        rows_of[pl.ds(d * (2 * MSG) + STATE_ROWS, OBS_ROWS), :] = even_rows
        rows_of[pl.ds(d * (2 * MSG) + MSG + STATE_ROWS, OBS_ROWS), :] = odd_rows
        return 0

    lax.fori_loop(0, NDEV // 2, fill, 0, unroll=8)


def field_kernel(me_ref, owner_ref, offset_ref, value_ref, error_ref, rank_ref, field_ref):
    odd_device = me_ref[0] % 2 == 1
    row_owner = owner_of_row()
    slot = iota((8, NOBS), 0).astype(F32)
    for b in range(2):
        hot = jnp.concatenate(
            [
                jnp.where(owner_ref[b : b + 1, t * LANES : (t + 1) * LANES] == row_owner, 1.0, 0.0).astype(BF16)
                for t in range(NOBS // LANES)
            ],
            axis=1,
        )
        here = rank_ref[b : b + 1, :] == slot
        rows = []
        for x in (offset_ref[b : b + 1, :].astype(F32), value_ref[b : b + 1, :], error_ref[b : b + 1, :]):
            rest = x
            for _ in range(3):
                part = rest.astype(BF16).astype(F32)
                rows.append(jnp.where(here, part, 0.0).astype(BF16))
                rest = rest - part
        t = lax.dot_general(
            jnp.concatenate(rows, axis=0), hot, (((1,), (1,)), ((), ())), preferred_element_type=F32
        )
        for f in range(3):
            at = f * 24
            even, odd = by_parity((t[at : at + 8] + t[at + 8 : at + 16]) + t[at + 16 : at + 24])
            same = jnp.where(odd_device, odd, even)
            other = jnp.where(odd_device, even, odd)
            field_ref[(b * 3 + f) * 8 : (b * 3 + f) * 8 + 8, :] = jnp.concatenate([same, other], axis=0)


def columns(row):
    return jnp.broadcast_to(row, (LANES, LANES)).T


def stats(raw, value, error):
    mean = jnp.sum(raw, axis=0, keepdims=True) * (1.0 / MEMBERS)
    anom = raw - mean
    varian = jnp.sum(anom * anom, axis=0, keepdims=True) * (1.0 / (MEMBERS - 1)) + 1e-06
    total = varian + error
    shrink = jnp.sqrt(error / total)
    scale = -1.0 / ((MEMBERS - 1) * total * (1.0 + shrink))
    push = anom - (value - mean) * (1.0 + shrink)
    return anom, anom * scale, push


def owner_weights(me_ref, table_ref):
    table8 = jnp.broadcast_to(table_ref[...], (8, LANES))
    par = me_ref[0] % 2
    delta = me_ref[0] // 2 - iota((8, LANES), 1) % 64
    steps = jnp.abs(delta)
    far = jnp.take_along_axis(table8, steps, axis=1)[0:1]
    near = jnp.take_along_axis(table8, jnp.maximum(steps - 1, 0), axis=1)[0:1]
    other = jnp.take_along_axis(table8, jnp.abs(2 * delta + 2 * par - 1) // 2, axis=1)[0:1]
    ahead = delta[0:1] > 0
    return jnp.where(ahead, near, far), jnp.where(ahead, far, near), jnp.where(ahead, 0.0, 1.0), other


def field(field_ref, b, f, lo, hi):
    base = (b * 3 + f) * 8
    return jnp.concatenate([field_ref[base + i : base + i + 1, :] for i in range(lo, hi)], axis=1)


def obs_columns(ref, stride, first, b):
    return jnp.concatenate(
        [
            jnp.concatenate(
                [ref[pl.ds(first + r * 8 + b * 4 + s, NDEV, stride=stride), :] for r in range(2)], axis=0
            )
            for s in range(4)
        ],
        axis=1,
    )


def state_columns(recv_ref, at):
    return jnp.concatenate(
        [
            jnp.concatenate(
                [recv_ref[pl.ds((at + h) * 2 + r, NDEV, stride=MSG), :] for r in range(2)], axis=0
            )
            for h in range(WIDE // LANES)
        ],
        axis=1,
    )


def centre(raw):
    return raw - jnp.sum(raw, axis=0, keepdims=True) * (1.0 / MEMBERS)


def same_gain(cov, at, thr, low, high):
    pieces = []
    for k in range(4):
        line = []
        for h in range(WIDE // LANES):
            c = cov[k * LANES : (k + 1) * LANES, h * LANES : (h + 1) * LANES]
            place = (iota((LANES, LANES), 1) + (at + h) * LANES).astype(F32)
            line.append(c * jnp.where(place >= thr[k * LANES : (k + 1) * LANES, :], high, low))
        pieces.append(jnp.concatenate(line, axis=1))
    return split(jnp.concatenate(pieces, axis=0))


def first_kernel(me_ref, table_ref, field_ref, recv_ref, new_ref, left_hi, left_lo, push_hi, push_lo, thr, low, high):
    w_low, w_high, shift, _ = owner_weights(me_ref, table_ref)
    low[...] = columns(w_low)
    high[...] = columns(w_high)
    _, scaled, push = stats(
        obs_columns(recv_ref, MSG, STATE_ROWS, 0), field(field_ref, 0, 1, 0, 4), field(field_ref, 0, 2, 0, 4)
    )
    left_hi[...], left_lo[...] = split(scaled.T)
    push_hi[...], push_lo[...] = split(push)
    off = field(field_ref, 0, 0, 0, 4)
    for s in range(4):
        thr[s * LANES : (s + 1) * LANES, :] = columns(off[:, s * LANES : (s + 1) * LANES] + shift)

    def tile(t, _):
        at = t * (WIDE // LANES)
        raw = state_columns(recv_ref, at)
        cov = dot3((left_hi[...], left_lo[...]), split(centre(raw)))
        gain = same_gain(cov, at, thr, low[...], high[...])
        raw = raw + dot3((push_hi[...], push_lo[...]), gain)
        new_ref[:, pl.ds(pl.multiple_of(t * WIDE, WIDE), WIDE)] = raw
        return 0

    lax.fori_loop(0, NV_DEV // WIDE, tile, 0, unroll=2)


def main_kernel(
    me_ref, table_ref, field_ref, recv_ref, other_ref, new_ref, out_ref,
    left_hi, left_lo, push_hi, push_lo, const_hi, const_lo, thr, low, high, off_col, raw2,
):
    par = me_ref[0] % 2
    table = jnp.broadcast_to(table_ref[...], (LANES, LANES))
    w_low, w_high, shift, w_other = owner_weights(me_ref, table_ref)
    w_other4 = jnp.concatenate([w_other] * 4, axis=1)

    def load_obs(b):
        return jnp.concatenate(
            [obs_columns(recv_ref, MSG, STATE_ROWS, b), obs_columns(other_ref, OBS_ROWS, 0, b)], axis=1
        )

    def block_setup(b, raw):
        _, scaled, push = stats(raw, field(field_ref, b, 1, 0, 8), field(field_ref, b, 2, 0, 8))
        left_hi[...], left_lo[...] = split(scaled.T)
        ph, pw = split(push)
        push_hi[...] = ph
        push_lo[...] = pw
        weighted = split(scaled[:, HALF:] * w_other4)
        const = dot3((ph[:, HALF:], pw[:, HALF:]), weighted, (((1,), (1,)), ((), ())))
        const_hi[b, :, :], const_lo[b, :, :] = split(const)

    low[...] = columns(w_low)
    high[...] = columns(w_high)
    off1 = field(field_ref, 0, 0, 0, 8)
    off2 = field(field_ref, 1, 0, 0, 8)
    for s in range(8):
        off_col[s * LANES : (s + 1) * LANES, :] = columns(off1[:, s * LANES : (s + 1) * LANES])
    for s in range(4):
        thr[s * LANES : (s + 1) * LANES, :] = columns(off2[:, s * LANES : (s + 1) * LANES] + shift)
    block_setup(0, load_obs(0))
    raw2[...] = load_obs(1)

    d = iota((LANES, LANES), 1) % 64 - iota((LANES, LANES), 0) % 64
    ad = jnp.abs(d)
    far = jnp.take_along_axis(table, ad, axis=1)
    near = jnp.take_along_axis(table, jnp.maximum(ad - 1, 0), axis=1)
    sign = jnp.where(d > 0, 1.0, jnp.where(d < 0, -1.0, 0.0))
    to_same = jnp.take_along_axis(table, jnp.abs(2 * d + 2 * par - 1) // 2, axis=1)
    to_other = jnp.take_along_axis(table, jnp.abs(2 * d + 1 - 2 * par) // 2, axis=1)
    for t in range(NOBS // OBS_WIDE):
        raw = raw2[:, t * OBS_WIDE : (t + 1) * OBS_WIDE]
        cov = dot3((left_hi[...], left_lo[...]), split(centre(raw)))
        in_same = t < NOBS // OBS_WIDE // 2
        pieces = []
        for k in range(8):
            line = []
            for h in range(OBS_WIDE // LANES):
                c = cov[k * LANES : (k + 1) * LANES, h * LANES : (h + 1) * LANES]
                if (k < 4) == in_same:
                    at = t * OBS_WIDE + h * LANES
                    gap = off2[:, at : at + LANES] - off_col[k * LANES : (k + 1) * LANES, :]
                    w = jnp.where(gap * sign >= 0.0, far, near)
                else:
                    w = to_same if in_same else to_other
                line.append(c * w)
            pieces.append(jnp.concatenate(line, axis=1))
        gain = split(jnp.concatenate(pieces, axis=0))
        raw2[:, t * OBS_WIDE : (t + 1) * OBS_WIDE] = raw + dot3((push_hi[...], push_lo[...]), gain)
    block_setup(1, raw2[...])

    def tile(t, _):
        at = t * (WIDE // LANES)
        before = split(centre(state_columns(recv_ref, at)))
        raw = new_ref[:, pl.ds(pl.multiple_of(t * WIDE, WIDE), WIDE)]
        raw = raw + dot3((const_hi[0], const_lo[0]), before)
        centred = split(centre(raw))
        cov = dot3((left_hi[0:HALF, :], left_lo[0:HALF, :]), centred)
        gain = same_gain(cov, at, thr, low[...], high[...])
        left = (
            jnp.concatenate([push_hi[:, 0:HALF], const_hi[1]], axis=1),
            jnp.concatenate([push_lo[:, 0:HALF], const_lo[1]], axis=1),
        )
        right = tuple(jnp.concatenate([g, c], axis=0) for g, c in zip(gain, centred))
        raw = raw + dot3(left, right)
        for h in range(WIDE // LANES):
            for r in range(2):
                out_ref[pl.ds((at + h) * 2 + r, NDEV, stride=STATE_ROWS), :] = raw[
                    r * NDEV : (r + 1) * NDEV, h * LANES : (h + 1) * LANES
                ]
        return 0

    lax.fori_loop(0, NV_DEV // WIDE, tile, 0, unroll=2)


VMEM = pl.BlockSpec(memory_space=pltpu.VMEM)
SMEM = pl.BlockSpec(memory_space=pltpu.SMEM)
HBM = pl.BlockSpec(memory_space=pltpu.HBM)


def params(mib):
    return pltpu.CompilerParams(vmem_limit_bytes=mib * 1024 * 1024)


def cost(flops, bytes_accessed):
    return pl.CostEstimate(flops=flops, bytes_accessed=bytes_accessed, transcendentals=0)


def prep(owner, offset, state):
    return pl.pallas_call(
        prep_kernel,
        out_shape=(
            jax.ShapeDtypeStruct((NDEV, MSG, LANES), F32),
            jax.ShapeDtypeStruct((2, NOBS), F32),
        ),
        in_specs=[HBM] * 3,
        out_specs=(VMEM, VMEM),
        scratch_shapes=[
            pltpu.VMEM((2, NOBS), jnp.int32),
            pltpu.VMEM((2, NOBS), jnp.int32),
            pltpu.SemaphoreType.DMA((3,)),
        ],
        compiler_params=params(60),
        name="prep",
    )(owner, offset, state)


def fields_of(me, owner, offset, value, error, rank):
    return pl.pallas_call(
        field_kernel,
        out_shape=jax.ShapeDtypeStruct((48, LANES), F32),
        in_specs=[SMEM] + [VMEM] * 5,
        out_specs=VMEM,
        compiler_params=params(16),
        cost_estimate=cost(2**27, 2**20),
        name="fields",
    )(me, owner, offset, value, error, rank)


def assimilate_first(me, table, fields, recv):
    return pl.pallas_call(
        first_kernel,
        out_shape=jax.ShapeDtypeStruct((MEMBERS, NV_DEV), F32),
        in_specs=[SMEM] + [VMEM] * 3,
        out_specs=VMEM,
        scratch_shapes=[
            pltpu.VMEM((HALF, MEMBERS), BF16),
            pltpu.VMEM((HALF, MEMBERS), BF16),
            pltpu.VMEM((MEMBERS, HALF), BF16),
            pltpu.VMEM((MEMBERS, HALF), BF16),
            pltpu.VMEM((HALF, LANES), F32),
            pltpu.VMEM((LANES, LANES), F32),
            pltpu.VMEM((LANES, LANES), F32),
        ],
        compiler_params=params(VMEM_MIB),
        cost_estimate=cost(3 * 2**31, 5 * 2**20),
        name="first",
    )(me, table, fields, recv)


def assimilate(me, table, fields, recv, other, new):
    return pl.pallas_call(
        main_kernel,
        out_shape=jax.ShapeDtypeStruct((NDEV * STATE_ROWS, LANES), F32),
        in_specs=[SMEM] + [VMEM] * 5,
        out_specs=VMEM,
        scratch_shapes=[
            pltpu.VMEM((NOBS, MEMBERS), BF16),
            pltpu.VMEM((NOBS, MEMBERS), BF16),
            pltpu.VMEM((MEMBERS, NOBS), BF16),
            pltpu.VMEM((MEMBERS, NOBS), BF16),
            pltpu.VMEM((2, MEMBERS, MEMBERS), BF16),
            pltpu.VMEM((2, MEMBERS, MEMBERS), BF16),
            pltpu.VMEM((HALF, LANES), F32),
            pltpu.VMEM((LANES, LANES), F32),
            pltpu.VMEM((LANES, LANES), F32),
            pltpu.VMEM((NOBS, LANES), F32),
            pltpu.VMEM((MEMBERS, NOBS), F32),
        ],
        compiler_params=params(VMEM_MIB),
        cost_estimate=cost(9 * 2**31, 9 * 2**20),
        name="assimilate",
    )(me, table, fields, recv, other, new)


def body(prior_state, obs_value, obs_error, obs_owner, obs_offset, taper_table):
    axes = ("mem", "var")
    me = lax.axis_index(axes).astype(jnp.int32).reshape(1)
    table = jnp.pad(taper_table, (0, LANES - taper_table.shape[0])).reshape(1, LANES)
    state = prior_state.reshape(2, NDEV * TILES, LANES).transpose(1, 0, 2).reshape(NDEV, STATE_ROWS, LANES)
    msg, rank = prep(obs_owner, obs_offset, state)
    recv = lax.all_to_all(msg, axes, split_axis=0, concat_axis=0, tiled=True)
    fields = fields_of(me, obs_owner, obs_offset, obs_value, obs_error, rank)
    mine = recv[:, STATE_ROWS:, :].reshape(NDEV * OBS_ROWS, LANES)
    other = lax.ppermute(mine, axes, [(i, i ^ 1) for i in range(NDEV)])
    recv = recv.reshape(NDEV * MSG, LANES)
    new = assimilate_first(me, table, fields, recv)
    new = assimilate(me, table, fields, recv, other, new)
    back = lax.all_to_all(
        new.reshape(NDEV, STATE_ROWS, LANES), axes, split_axis=0, concat_axis=0, tiled=True
    )
    rows = back.reshape(NDEV * TILES, 2, LANES).transpose(1, 0, 2)
    rows = with_layout_constraint(rows, Layout(major_to_minor=(1, 0, 2)))
    return rows.reshape(2, NDEV * NV_DEV)


def solution(mesh):
    in_specs = (P(("mem", "var"), None), P(), P(), P(), P(), P())
    out_specs = P(("mem", "var"), None)
    return jax.shard_map(body, mesh=mesh, in_specs=in_specs, out_specs=out_specs, check_vma=False)
```

time: 140 us -> 114 us (0.81)
  waiting for transfers between devices: 52.6 us -> 0.01 us
  blocking collectives: 34.4 us -> 86.5 us
  Pallas kernels: 35.1 us -> 23.7 us
  starting transfers between devices: 12 us -> 1.17 us
  local copies, waits for them, and re-layouts: 5.7 us -> 2.39 us
    all_to_all x0 -> x1, blocking collectives: none -> 53 us  [body(): recv = lax.all_to_all(msg, axes, split_axis=0, concat_axis=0, tiled=True)]
    all_to_all x1 -> x0, waiting for transfers between devices: 52.6 us -> none  [body(): lax.all_to_all(msg.reshape(NDEV, MSG, LANES), axes, split_axis=0, concat_...]
    pallas_call x1, Pallas kernels: 30.7 us -> 13.9 us  [assimilate(): pl.pallas_call(main_kernel, out_shape=jax.ShapeDtypeStruct((NDEV * STATE_...]
    all_to_all x1 -> x0, starting transfers between devices: 12 us -> none  [body(): lax.all_to_all(msg.reshape(NDEV, MSG, LANES), axes, split_axis=0, concat_...]
    pallas_call x1 -> x3, Pallas kernels: 4.39 us -> 9.81 us  [the longest x1 4.77 us: prep(): pl.pallas_call(prep_kernel, out_shape=(jax.ShapeDtypeStruct((NDEV, MSG, L...]
    unnamed x13, local copies, waits for them, and re-layouts: 5.7 us -> 1.34 us
  transfers between devices with their start and end apart: 1 -> 1, of which waited for: 1 -> 0; matrix products, arithmetic and copies ran while one was open for 0% -> 0% of each run, Pallas kernels for 0% -> 4%
where the time goes in v2:
time: 114 us
  blocking collectives  86.5 us (76%)
  Pallas kernels  23.7 us (21%)
  local copies, waits for them, and re-layouts  2.39 us (2%)
  starting transfers between devices  1.17 us (1%)
    all_to_all x1, blocking collectives, body(): recv = lax.all_to_all(msg, axes, split_axis=0, concat_axis=0, tiled=True)  53 us
    all_to_all x1, blocking collectives, body(): lax.all_to_all(new.reshape(NDEV, STATE_ROWS, LANES), axes, split_axis=0,...  33.5 us
    pallas_call x1, Pallas kernels, assimilate(): pl.pallas_call(main_kernel, out_shape=jax.ShapeDtypeStruct((NDEV * STATE_...  13.9 us
    pallas_call x1, Pallas kernels, prep(): pl.pallas_call(prep_kernel, out_shape=(jax.ShapeDtypeStruct((NDEV, MSG, L...  4.77 us
    pallas_call x1, Pallas kernels, assimilate_first(): pl.pallas_call(first_kernel, out_shape=jax.ShapeDtypeStruct((MEMBERS, NV_...  4.6 us
  transfers between devices with their start and end apart: 1, of which 0 were waited for; matrix products, arithmetic and copies ran while one was open for 0% of the time, Pallas kernels for 4%

profile of v2, /device:TPU:1, one launch (start us, length us, event | category | flops | bytes accessed | tf_op | source)
XLA Modules:
  0.0 113.8 jit_solution(4176781811930382686)
XLA Ops:
  0.0 4.8 %prep.1 = (f32[128,48,128]{2,1,0:T(8,128)}, f32[2,1024]{1,0:T(2,128)}) custom-call(s32[2,1024]{1,0:T(2,128)} %owner_ref.1, s32[2,1024]{1,0:T(2,128)} %offset_ref.1, f32[128,32,128]{2,1,0:T(8,128)} %bitcast.20), custom_call_target="tpu_custom_call" | custom-call | tf_op jit(solution)/shard_map/prep/pallas_call | solution.py:354
  4.8 53.0 %all_to_all.10 = f32[128,48,128]{2,1,0:T(8,128)S(1)} all-to-all(f32[128,48,128]{2,1,0:T(8,128)} %get-tuple-element.8), channel_id=1, replica_groups=mesh['mem'=4,'var'=32] {'mem','var'}, dimensions={0} | all-to-all | bytes 6291456 | tf_op jit(solution)/shard_map/all_to_all | solution.py:436
  57.8 0.0 copy-start
  57.8 0.0 copy-start.1
  57.8 0.0 copy-start.2
  57.8 0.0 copy-start.3
  57.8 0.0 copy-start.4
  57.8 0.0 copy-start.5
  57.8 1.0 slice.4
  58.9 1.2 %collective-permute-start = (f32[2048,128]{1,0:T(8,128)}, f32[2048,128]{1,0:T(8,128)}, u32[]{:S(2)}, u32[]{:S(2)}) collective-permute-start(f32[2048,128]{1,0:T(8,128)} %bitcast.6), channel_id=1, source_target_pairs={{0,1},{1,0},{2,3},{3,2},{4,5},{5,4},{6,7},{7,6},{8,9},{9,8},{10,11... | collective-permute-start | bytes 3145736 | tf_op jit(solution)/shard_map/ppermute | solution.py:439
  60.1 0.0 copy-done
  60.1 0.0 copy-done.1
  60.1 0.0 copy-done.2
  60.1 0.0 copy-done.3
  60.1 0.0 copy-done.4
  60.1 0.4 fields.1.field_ref
  60.5 0.0 copy-done.5
  60.5 4.6 %first.1.new_ref = f32[256,2048]{1,0:T(8,128)S(1)} custom-call(s32[1]{0:T(128)} %bitcast.me_ref, f32[1,128]{1,0:T(1,128)S(1)} %pad_bitcast_fusion.table_ref, f32[48,128]{1,0:T(8,128)S(1)} %fields.1.field_ref, f32[6144,128]{1,0:T(8,128)S(1)} %bitcast.16), custom_call_target="tpu_custom_call" | custom-call | flops 6442450944 | bytes 5242880 | tf_op jit(solution)/shard_map/first/pallas_call | solution.py:385
  65.1 0.0 collective-permute-done.other_ref
  65.2 13.9 %assimilate.1 = f32[4096,128]{1,0:T(8,128)S(1)} custom-call(s32[1]{0:T(128)} %bitcast.me_ref, f32[1,128]{1,0:T(1,128)S(1)} %pad_bitcast_fusion.table_ref, f32[48,128]{1,0:T(8,128)S(1)} %fields.1.field_ref, f32[6144,128]{1,0:T(8,128)S(1)} %bitcast.17, f32[2048,128]{1,0:T(8,128)} %collective-permute-done.other_ref, f32[256,2048]{1,0:T(8,128)S(1)} %first.1.new_ref), custom_call_target="tpu_custom_call" | custom-call | flops 19327352832 | bytes 9437184 | tf_op jit(solution)/shard_map/assimilate/pallas_call | solution.py:406
  79.0 33.5 %all_to_all.11 = f32[128,32,128]{2,1,0:T(8,128)S(1)} all-to-all(f32[128,32,128]{2,1,0:T(8,128)S(1)} %bitcast.18), channel_id=1, replica_groups=mesh['mem'=4,'var'=32] {'mem','var'}, dimensions={0} | all-to-all | bytes 4194304 | tf_op jit(solution)/shard_map/all_to_all | solution.py:443
  112.5 1.3 %copy.9 = f32[2,262144]{1,0:T(2,128)} copy(f32[2,262144]{1,0:T(2,128)S(1)} %bitcast.19) | data formatting | bytes 4194304
  (1 shorter events, 0.0 us)
Async XLA Ops:
  57.8 2.2 %copy-start = (s32[2,1024]{1,0:T(2,128)S(1)}, s32[2,1024]{1,0:T(2,128)}, u32[]{:S(2)}) copy-start(s32[2,1024]{1,0:T(2,128)} %owner_ref.1) | copy-start | bytes 24580
  57.8 2.2 %copy-start.1 = (s32[2,1024]{1,0:T(2,128)S(1)}, s32[2,1024]{1,0:T(2,128)}, u32[]{:S(2)}) copy-start(s32[2,1024]{1,0:T(2,128)} %offset_ref.1) | copy-start | bytes 24580
  57.8 2.2 %copy-start.2 = (f32[2,1024]{1,0:T(2,128)S(1)}, f32[2,1024]{1,0:T(2,128)}, u32[]{:S(2)}) copy-start(f32[2,1024]{1,0:T(2,128)} %value_ref.1) | copy-start | bytes 24580
  57.8 2.2 %copy-start.3 = (f32[2,1024]{1,0:T(2,128)S(1)}, f32[2,1024]{1,0:T(2,128)}, u32[]{:S(2)}) copy-start(f32[2,1024]{1,0:T(2,128)} %error_ref.1) | copy-start | bytes 24580
  57.8 2.2 %copy-start.4 = (f32[2,1024]{1,0:T(2,128)S(1)}, f32[2,1024]{1,0:T(2,128)}, u32[]{:S(2)}) copy-start(f32[2,1024]{1,0:T(2,128)} %get-tuple-element.7.rank_ref) | copy-start | bytes 24580
  57.8 2.7 %copy-start.5 = (f32[64]{0:T(128)S(1)}, f32[64]{0:T(128)}, u32[]{:S(2)}) copy-start(f32[64]{0:T(128)} %param.11) | copy-start | bytes 772
  58.9 6.3 %collective-permute-start = (f32[2048,128]{1,0:T(8,128)}, f32[2048,128]{1,0:T(8,128)}, u32[]{:S(2)}, u32[]{:S(2)}) collective-permute-start(f32[2048,128]{1,0:T(8,128)} %bitcast.6), channel_id=1, source_target_pairs={{0,1},{1,0},{2,3},{3,2},{4,5},{5,4},{6,7},{7,6},{8,9},{9,8},{10,11... | collective-permute-start | bytes 3145736 | tf_op jit(solution)/shard_map/ppermute | solution.py:439

commit v3 on v2

--- a/solution.py
+++ b/solution.py
@@ -18,6 +18,7 @@
 STATE_ROWS = 2 * TILES
 OBS_ROWS = 16
 MSG = STATE_ROWS + OBS_ROWS
+PIECES = 4
 WIDE = 1024
 OBS_WIDE = 512
 F32 = jnp.float32
@@ -54,17 +55,28 @@
     return (2 * row) % LANES + row // 64
 
 
-def prep_kernel(owner_hbm, offset_hbm, state_hbm, msg_ref, rank_ref, owner_ref, offset_ref, sems):
+def prep_kernel(
+    me_ref, owner_hbm, offset_hbm, state_hbm, msg_ref, rank_ref, owner_ref, offset_ref, small_sems, state_sems
+):
     rows_of = msg_ref.reshape(NDEV * MSG, LANES)
-    state_copy = pltpu.make_async_copy(state_hbm, msg_ref.at[:, 0:STATE_ROWS, :], sems.at[0])
-    owner_copy = pltpu.make_async_copy(owner_hbm, owner_ref, sems.at[1])
-    offset_copy = pltpu.make_async_copy(offset_hbm, offset_ref, sems.at[2])
+    owner_copy = pltpu.make_async_copy(owner_hbm, owner_ref, small_sems.at[0])
+    offset_copy = pltpu.make_async_copy(offset_hbm, offset_ref, small_sems.at[1])
     owner_copy.start()
     offset_copy.start()
-    state_copy.start()
+    share = NDEV // PIECES
+    pieces = [
+        pltpu.make_async_copy(
+            state_hbm.at[p * share : (p + 1) * share],
+            msg_ref.at[p * share : (p + 1) * share, 0:STATE_ROWS, :],
+            state_sems.at[p],
+        )
+        for p in range(PIECES)
+    ]
+    for piece in pieces:
+        piece.start()
     owner_copy.wait()
     offset_copy.wait()
-    row_owner = owner_of_row()
+    row_owner = iota((LANES, LANES), 0)
     before = jnp.where(iota((LANES, LANES), 0) < iota((LANES, LANES), 1), 1.0, 0.0).astype(BF16)
     slot = iota((8, NOBS), 0).astype(F32)
     tables = []
@@ -92,37 +104,37 @@
     pad = jnp.zeros((LANES - 16, LANES), F32)
     tile_of = jnp.concatenate([tables[0][0:8], tables[1][0:8], pad], axis=0).T.astype(jnp.int32)
     lane_of = jnp.concatenate([tables[0][8:16], tables[1][8:16], pad], axis=0).T.astype(jnp.int32)
-    state_copy.wait()
+    groups = [[], []]
+    for g in range(NDEV // 8):
+        if g % (share // 8) == 0:
+            pieces[g // (share // 8)].wait()
+        want_tile = tile_of[g * 8 : g * 8 + 8, :]
+        want_lane = lane_of[g * 8 : g * 8 + 8, :]
+        for r in range(2):
+            acc = jnp.zeros((8, LANES), F32)
+            for c in range(TILES):
+                x = rows_of[pl.ds(g * 8 * MSG + c * 2 + r, 8, stride=MSG), :]
+                acc = jnp.where(want_tile == c, jnp.take_along_axis(x, want_lane, axis=1), acc)
+            groups[r].append(acc)
+    lane = iota((8, LANES), 1)
+    parity_order = (2 * lane) % LANES + lane // 64
     even_rows = []
     odd_rows = []
     for r in range(2):
-        groups = []
-        for g in range(16):
-            want_tile = tile_of[g * 8 : g * 8 + 8, :]
-            want_lane = lane_of[g * 8 : g * 8 + 8, :]
-            first = 16 * g if g < 8 else 16 * (g - 8) + 1
-            acc = jnp.zeros((8, LANES), F32)
-            for c in range(TILES):
-                x = rows_of[pl.ds(first * MSG + c * 2 + r, 8, stride=2 * MSG), :]
-                acc = jnp.where(want_tile == c, jnp.take_along_axis(x, want_lane, axis=1), acc)
-            groups.append(acc)
-        found = jnp.concatenate(groups, axis=0).T
+        found = jnp.concatenate(groups[r], axis=0).T
         for b in range(2):
-            even, odd = by_parity(found[b * 8 : b * 8 + 8])
+            even, odd = by_parity(jnp.take_along_axis(found[b * 8 : b * 8 + 8], parity_order, axis=1))
             even_rows.append(even)
             odd_rows.append(odd)
     even_rows = jnp.concatenate(even_rows, axis=0)
     odd_rows = jnp.concatenate(odd_rows, axis=0)
-
-    def fill(d, _):
-        rows_of[pl.ds(d * (2 * MSG) + STATE_ROWS, OBS_ROWS), :] = even_rows
-        rows_of[pl.ds(d * (2 * MSG) + MSG + STATE_ROWS, OBS_ROWS), :] = odd_rows
-        return 0
-
-    lax.fori_loop(0, NDEV // 2, fill, 0, unroll=8)
-
-
-def field_kernel(me_ref, owner_ref, offset_ref, value_ref, error_ref, rank_ref, field_ref):
+    for d in range(NDEV):
+        msg_ref[d, STATE_ROWS:MSG, :] = odd_rows if d % 2 else even_rows
+
+
+def field_kernel(me_ref, owner_ref, offset_ref, value_ref, error_ref, rank_ref, recv_ref, mine_ref, field_ref):
+    for d in range(NDEV):
+        mine_ref[d, :, :] = recv_ref[d, STATE_ROWS:MSG, :]
     odd_device = me_ref[0] % 2 == 1
     row_owner = owner_of_row()
     slot = iota((8, NOBS), 0).astype(F32)
@@ -207,10 +219,6 @@
         ],
         axis=1,
     )
-
-
-def centre(raw):
-    return raw - jnp.sum(raw, axis=0, keepdims=True) * (1.0 / MEMBERS)
 
 
 def same_gain(cov, at, thr, low, high):
@@ -241,7 +249,7 @@
     def tile(t, _):
         at = t * (WIDE // LANES)
         raw = state_columns(recv_ref, at)
-        cov = dot3((left_hi[...], left_lo[...]), split(centre(raw)))
+        cov = dot3((left_hi[...], left_lo[...]), split(raw))
         gain = same_gain(cov, at, thr, low[...], high[...])
         raw = raw + dot3((push_hi[...], push_lo[...]), gain)
         new_ref[:, pl.ds(pl.multiple_of(t * WIDE, WIDE), WIDE)] = raw
@@ -294,7 +302,7 @@
     to_other = jnp.take_along_axis(table, jnp.abs(2 * d + 1 - 2 * par) // 2, axis=1)
     for t in range(NOBS // OBS_WIDE):
         raw = raw2[:, t * OBS_WIDE : (t + 1) * OBS_WIDE]
-        cov = dot3((left_hi[...], left_lo[...]), split(centre(raw)))
+        cov = dot3((left_hi[...], left_lo[...]), split(raw))
         in_same = t < NOBS // OBS_WIDE // 2
         pieces = []
         for k in range(8):
@@ -315,10 +323,10 @@
 
     def tile(t, _):
         at = t * (WIDE // LANES)
-        before = split(centre(state_columns(recv_ref, at)))
+        before = split(state_columns(recv_ref, at))
         raw = new_ref[:, pl.ds(pl.multiple_of(t * WIDE, WIDE), WIDE)]
         raw = raw + dot3((const_hi[0], const_lo[0]), before)
-        centred = split(centre(raw))
+        centred = split(raw)
         cov = dot3((left_hi[0:HALF, :], left_lo[0:HALF, :]), centred)
         gain = same_gain(cov, at, thr, low[...], high[...])
         left = (
@@ -350,35 +358,42 @@
     return pl.CostEstimate(flops=flops, bytes_accessed=bytes_accessed, transcendentals=0)
 
 
-def prep(owner, offset, state):
+def in_hbm(x):
+    return pltpu.with_memory_space_constraint(x, pltpu.HBM)
+
+
+def prep(me, owner, offset, state):
     return pl.pallas_call(
         prep_kernel,
         out_shape=(
             jax.ShapeDtypeStruct((NDEV, MSG, LANES), F32),
             jax.ShapeDtypeStruct((2, NOBS), F32),
         ),
-        in_specs=[HBM] * 3,
+        in_specs=[SMEM] + [HBM] * 3,
         out_specs=(VMEM, VMEM),
         scratch_shapes=[
             pltpu.VMEM((2, NOBS), jnp.int32),
             pltpu.VMEM((2, NOBS), jnp.int32),
-            pltpu.SemaphoreType.DMA((3,)),
+            pltpu.SemaphoreType.DMA((2,)),
+            pltpu.SemaphoreType.DMA((PIECES,)),
         ],
-        compiler_params=params(60),
+        compiler_params=params(16),
         name="prep",
-    )(owner, offset, state)
-
-
-def fields_of(me, owner, offset, value, error, rank):
+    )(me, owner, offset, state)
+
+
+def sort_out(me, owner, offset, value, error, rank, recv):
     return pl.pallas_call(
         field_kernel,
-        out_shape=jax.ShapeDtypeStruct((48, LANES), F32),
-        in_specs=[SMEM] + [VMEM] * 5,
-        out_specs=VMEM,
+        out_shape=(
+            jax.ShapeDtypeStruct((NDEV, OBS_ROWS, LANES), F32),
+            jax.ShapeDtypeStruct((48, LANES), F32),
+        ),
+        in_specs=[SMEM] + [VMEM] * 6,
+        out_specs=(VMEM, VMEM),
         compiler_params=params(16),
-        cost_estimate=cost(2**27, 2**20),
         name="fields",
-    )(me, owner, offset, value, error, rank)
+    )(me, owner, offset, value, error, rank, recv)
 
 
 def assimilate_first(me, table, fields, recv):
@@ -430,13 +445,12 @@
 def body(prior_state, obs_value, obs_error, obs_owner, obs_offset, taper_table):
     axes = ("mem", "var")
     me = lax.axis_index(axes).astype(jnp.int32).reshape(1)
+    state = prior_state.reshape(2, NDEV * TILES, LANES).transpose(1, 0, 2).reshape(NDEV, STATE_ROWS, LANES)
+    msg, rank = prep(me, in_hbm(obs_owner), in_hbm(obs_offset), in_hbm(state))
+    recv = lax.all_to_all(msg, axes, split_axis=0, concat_axis=0, tiled=True)
     table = jnp.pad(taper_table, (0, LANES - taper_table.shape[0])).reshape(1, LANES)
-    state = prior_state.reshape(2, NDEV * TILES, LANES).transpose(1, 0, 2).reshape(NDEV, STATE_ROWS, LANES)
-    msg, rank = prep(obs_owner, obs_offset, state)
-    recv = lax.all_to_all(msg, axes, split_axis=0, concat_axis=0, tiled=True)
-    fields = fields_of(me, obs_owner, obs_offset, obs_value, obs_error, rank)
-    mine = recv[:, STATE_ROWS:, :].reshape(NDEV * OBS_ROWS, LANES)
-    other = lax.ppermute(mine, axes, [(i, i ^ 1) for i in range(NDEV)])
+    mine, fields = sort_out(me, obs_owner, obs_offset, obs_value, obs_error, rank, recv)
+    other = lax.ppermute(mine, axes, [(i, i ^ 1) for i in range(NDEV)]).reshape(NDEV * OBS_ROWS, LANES)
     recv = recv.reshape(NDEV * MSG, LANES)
     new = assimilate_first(me, table, fields, recv)
     new = assimilate(me, table, fields, recv, other, new)

time: 114 us -> 109 us (0.956)
  Pallas kernels: 23.7 us -> 20 us
    pallas_call x1, Pallas kernels: 13.9 us -> 12.1 us  [assimilate(): pl.pallas_call(main_kernel, out_shape=jax.ShapeDtypeStruct((NDEV * STATE_...]
    pallas_call x1, Pallas kernels: 4.77 us -> 3.15 us  [prep(): pl.pallas_call(prep_kernel, out_shape=(jax.ShapeDtypeStruct((NDEV, MSG, L...]
where the time goes in v3:
time: 109 us
  blocking collectives  86.3 us (79%)
  Pallas kernels  20 us (18%)
  starting transfers between devices  1.43 us (1%)
  local copies, waits for them, and re-layouts  1.35 us (1%)
    all_to_all x1, blocking collectives, body(): recv = lax.all_to_all(msg, axes, split_axis=0, concat_axis=0, tiled=True)  52.8 us
    all_to_all x1, blocking collectives, body(): lax.all_to_all(new.reshape(NDEV, STATE_ROWS, LANES), axes, split_axis=0,...  33.5 us
    pallas_call x1, Pallas kernels, assimilate(): pl.pallas_call(main_kernel, out_shape=jax.ShapeDtypeStruct((NDEV * STATE_...  12.1 us
    pallas_call x1, Pallas kernels, assimilate_first(): pl.pallas_call(first_kernel, out_shape=jax.ShapeDtypeStruct((MEMBERS, NV_...  4.33 us
    pallas_call x1, Pallas kernels, prep(): pl.pallas_call(prep_kernel, out_shape=(jax.ShapeDtypeStruct((NDEV, MSG, L...  3.15 us
  transfers between devices with their start and end apart: 1, of which 0 were waited for; matrix products, arithmetic and copies ran while one was open for 0% of the time, Pallas kernels for 4%

profile of v3, /device:TPU:1, one launch (start us, length us, event | category | flops | bytes accessed | tf_op | source)
XLA Modules:
  0.0 109.2 jit_solution(17065500608276975471)
XLA Ops:
  0.0 3.1 %prep.1 = (f32[128,48,128]{2,1,0:T(8,128)S(1)}, f32[2,1024]{1,0:T(2,128)S(1)}) custom-call(s32[1]{0:T(128)} %bitcast.me_ref, s32[2,1024]{1,0:T(2,128)} %owner_ref.1, s32[2,1024]{1,0:T(2,128)} %offset_ref.1, f32[128,32,128]{2,1,0:T(8,128)} %bitcast.21), custom_call_target="tpu_custom_call" | custom-call | tf_op jit(solution)/shard_map/prep/pallas_call | solution.py:366
  3.2 0.0 copy-start
  3.2 0.0 copy-start.1
  3.2 0.0 copy-start.2
  3.2 0.0 copy-start.3
  3.2 52.8 %all_to_all.10.recv_ref = f32[128,48,128]{2,1,0:T(8,128)S(1)} all-to-all(f32[128,48,128]{2,1,0:T(8,128)S(1)} %get-tuple-element.10), channel_id=1, replica_groups=mesh['mem'=4,'var'=32] {'mem','var'}, dimensions={0} | all-to-all | bytes 6291456 | tf_op jit(solution)/shard_map/all_to_all | solution.py:450
  56.0 0.0 copy-start.4
  56.0 0.0 copy-done
  56.0 0.0 copy-done.1
  56.0 0.0 copy-done.2
  56.0 0.0 copy-done.3
  56.1 0.5 fields.1
  56.5 1.4 %collective-permute-start = (f32[128,16,128]{2,1,0:T(8,128)S(1)}, f32[128,16,128]{2,1,0:T(8,128)S(1)}, u32[]{:S(2)}, u32[]{:S(2)}) collective-permute-start(f32[128,16,128]{2,1,0:T(8,128)S(1)} %get-tuple-element.12), channel_id=1, source_target_pairs={{0,1},{1,0},{2,3},{3,2},{4,5},{5,4},{6,7},{7,6},{8,9},{9,8},{10,11... | collective-permute-start | bytes 3145736 | tf_op jit(solution)/shard_map/ppermute | solution.py:453
  58.0 0.0 copy-done.4
  58.0 4.3 %first.1.new_ref = f32[256,2048]{1,0:T(8,128)S(1)} custom-call(s32[1]{0:T(128)} %bitcast.me_ref, f32[1,128]{1,0:T(1,128)S(1)} %pad_bitcast_fusion.table_ref, f32[48,128]{1,0:T(8,128)S(1)} %get-tuple-element.11.field_ref, f32[6144,128]{1,0:T(8,128)S(1)} %bitcast.16), custom_call_target="tpu_custom_call" | custom-call | flops 6442450944 | bytes 5242880 | tf_op jit(solution)/shard_map/first/pallas_call | solution.py:400
  62.3 0.0 collective-permute-done
  62.3 12.1 %assimilate.1 = f32[4096,128]{1,0:T(8,128)S(1)} custom-call(s32[1]{0:T(128)} %bitcast.me_ref, f32[1,128]{1,0:T(1,128)S(1)} %pad_bitcast_fusion.table_ref, f32[48,128]{1,0:T(8,128)S(1)} %get-tuple-element.11.field_ref, f32[6144,128]{1,0:T(8,128)S(1)} %bitcast.17, f32[2048,128]{1,0:T(8,128)S(1)} %bitcast.19, f32[256,2048]{1,0:T(8,128)S(1)} %first.1.new_ref), custom_call_target="tpu_custom_call" | custom-call | flops 19327352832 | bytes 9437184 | tf_op jit(solution)/shard_map/assimilate/pallas_call | solution.py:421
  74.4 33.5 %all_to_all.11 = f32[128,32,128]{2,1,0:T(8,128)S(1)} all-to-all(f32[128,32,128]{2,1,0:T(8,128)S(1)} %bitcast.18), channel_id=1, replica_groups=mesh['mem'=4,'var'=32] {'mem','var'}, dimensions={0} | all-to-all | bytes 4194304 | tf_op jit(solution)/shard_map/all_to_all | solution.py:457
  107.9 1.3 %copy.9 = f32[2,262144]{1,0:T(2,128)} copy(f32[2,262144]{1,0:T(2,128)S(1)} %bitcast.20) | data formatting | bytes 4194304
  (1 shorter events, 0.0 us)
Async XLA Ops:
  3.2 52.9 %copy-start = (s32[2,1024]{1,0:T(2,128)S(1)}, s32[2,1024]{1,0:T(2,128)}, u32[]{:S(2)}) copy-start(s32[2,1024]{1,0:T(2,128)} %owner_ref.1) | copy-start | bytes 24580
  3.2 52.9 %copy-start.1 = (s32[2,1024]{1,0:T(2,128)S(1)}, s32[2,1024]{1,0:T(2,128)}, u32[]{:S(2)}) copy-start(s32[2,1024]{1,0:T(2,128)} %offset_ref.1) | copy-start | bytes 24580
  3.2 52.9 %copy-start.2 = (f32[2,1024]{1,0:T(2,128)S(1)}, f32[2,1024]{1,0:T(2,128)}, u32[]{:S(2)}) copy-start(f32[2,1024]{1,0:T(2,128)} %value_ref.1) | copy-start | bytes 24580
  3.2 52.9 %copy-start.3 = (f32[2,1024]{1,0:T(2,128)S(1)}, f32[2,1024]{1,0:T(2,128)}, u32[]{:S(2)}) copy-start(f32[2,1024]{1,0:T(2,128)} %error_ref.1) | copy-start | bytes 24580
  56.0 1.9 %copy-start.4 = (f32[64]{0:T(128)S(1)}, f32[64]{0:T(128)}, u32[]{:S(2)}) copy-start(f32[64]{0:T(128)} %param.11) | copy-start | bytes 772
  56.5 5.8 %collective-permute-start = (f32[128,16,128]{2,1,0:T(8,128)S(1)}, f32[128,16,128]{2,1,0:T(8,128)S(1)}, u32[]{:S(2)}, u32[]{:S(2)}) collective-permute-start(f32[128,16,128]{2,1,0:T(8,128)S(1)} %get-tuple-element.12), channel_id=1, source_target_pairs={{0,1},{1,0},{2,3},{3,2},{4,5},{5,4},{6,7},{7,6},{8,9},{9,8},{10,11... | collective-permute-start | bytes 3145736 | tf_op jit(solution)/shard_map/ppermute | solution.py:453

commit v4 on v3

--- a/solution.py
+++ b/solution.py
@@ -18,9 +18,8 @@
 STATE_ROWS = 2 * TILES
 OBS_ROWS = 16
 MSG = STATE_ROWS + OBS_ROWS
-PIECES = 4
+PIECES = 1
 WIDE = 1024
-OBS_WIDE = 512
 F32 = jnp.float32
 BF16 = jnp.bfloat16
 VMEM_MIB = 32
@@ -33,6 +32,9 @@
 def split(x):
     hi = x.astype(BF16)
     return hi, (x - hi.astype(F32)).astype(BF16)
+
+
+BOTH_LANES = (((1,), (1,)), ((), ()))
 
 
 def dot3(a, b, dims=(((1,), (0,)), ((), ()))):
@@ -233,7 +235,9 @@
     return split(jnp.concatenate(pieces, axis=0))
 
 
-def first_kernel(me_ref, table_ref, field_ref, recv_ref, new_ref, left_hi, left_lo, push_hi, push_lo, thr, low, high):
+def first_kernel(
+    me_ref, table_ref, field_ref, recv_ref, new_ref, left_hi, left_lo, push_hi, push_lo, low, high, thr
+):
     w_low, w_high, shift, _ = owner_weights(me_ref, table_ref)
     low[...] = columns(w_low)
     high[...] = columns(w_high)
@@ -246,53 +250,31 @@
     for s in range(4):
         thr[s * LANES : (s + 1) * LANES, :] = columns(off[:, s * LANES : (s + 1) * LANES] + shift)
 
-    def tile(t, _):
+    for t in range(NV_DEV // WIDE):
         at = t * (WIDE // LANES)
         raw = state_columns(recv_ref, at)
         cov = dot3((left_hi[...], left_lo[...]), split(raw))
         gain = same_gain(cov, at, thr, low[...], high[...])
         raw = raw + dot3((push_hi[...], push_lo[...]), gain)
-        new_ref[:, pl.ds(pl.multiple_of(t * WIDE, WIDE), WIDE)] = raw
-        return 0
-
-    lax.fori_loop(0, NV_DEV // WIDE, tile, 0, unroll=2)
+        new_ref[:, t * WIDE : (t + 1) * WIDE] = raw
 
 
 def main_kernel(
-    me_ref, table_ref, field_ref, recv_ref, other_ref, new_ref, out_ref,
-    left_hi, left_lo, push_hi, push_lo, const_hi, const_lo, thr, low, high, off_col, raw2,
+    me_ref, table_ref, field_ref, recv_ref, other_ref, new_ref,
+    first_left_hi, first_left_lo, first_push_hi, first_push_lo, low, high, out_ref,
+    left_hi, left_lo, push_hi, push_lo, left2_hi, left2_lo, push2_hi, push2_lo, const_hi, const_lo, thr,
 ):
     par = me_ref[0] % 2
     table = jnp.broadcast_to(table_ref[...], (LANES, LANES))
-    w_low, w_high, shift, w_other = owner_weights(me_ref, table_ref)
+    _, _, shift, w_other = owner_weights(me_ref, table_ref)
     w_other4 = jnp.concatenate([w_other] * 4, axis=1)
 
-    def load_obs(b):
-        return jnp.concatenate(
-            [obs_columns(recv_ref, MSG, STATE_ROWS, b), obs_columns(other_ref, OBS_ROWS, 0, b)], axis=1
-        )
-
-    def block_setup(b, raw):
-        _, scaled, push = stats(raw, field(field_ref, b, 1, 0, 8), field(field_ref, b, 2, 0, 8))
-        left_hi[...], left_lo[...] = split(scaled.T)
-        ph, pw = split(push)
-        push_hi[...] = ph
-        push_lo[...] = pw
-        weighted = split(scaled[:, HALF:] * w_other4)
-        const = dot3((ph[:, HALF:], pw[:, HALF:]), weighted, (((1,), (1,)), ((), ())))
+    def set_const(b, scaled, push):
+        const = dot3(push, split(scaled * w_other4), BOTH_LANES)
         const_hi[b, :, :], const_lo[b, :, :] = split(const)
 
-    low[...] = columns(w_low)
-    high[...] = columns(w_high)
     off1 = field(field_ref, 0, 0, 0, 8)
     off2 = field(field_ref, 1, 0, 0, 8)
-    for s in range(8):
-        off_col[s * LANES : (s + 1) * LANES, :] = columns(off1[:, s * LANES : (s + 1) * LANES])
-    for s in range(4):
-        thr[s * LANES : (s + 1) * LANES, :] = columns(off2[:, s * LANES : (s + 1) * LANES] + shift)
-    block_setup(0, load_obs(0))
-    raw2[...] = load_obs(1)
-
     d = iota((LANES, LANES), 1) % 64 - iota((LANES, LANES), 0) % 64
     ad = jnp.abs(d)
     far = jnp.take_along_axis(table, ad, axis=1)
@@ -300,38 +282,66 @@
     sign = jnp.where(d > 0, 1.0, jnp.where(d < 0, -1.0, 0.0))
     to_same = jnp.take_along_axis(table, jnp.abs(2 * d + 2 * par - 1) // 2, axis=1)
     to_other = jnp.take_along_axis(table, jnp.abs(2 * d + 1 - 2 * par) // 2, axis=1)
-    for t in range(NOBS // OBS_WIDE):
-        raw = raw2[:, t * OBS_WIDE : (t + 1) * OBS_WIDE]
-        cov = dot3((left_hi[...], left_lo[...]), split(raw))
-        in_same = t < NOBS // OBS_WIDE // 2
+
+    def alike(cov, first):
         pieces = []
-        for k in range(8):
+        for k in range(4):
+            at = first + k * LANES
+            column = columns(off1[:, at : at + LANES])
             line = []
-            for h in range(OBS_WIDE // LANES):
+            for h in range(4):
+                gap = off2[:, first + h * LANES : first + (h + 1) * LANES] - column
                 c = cov[k * LANES : (k + 1) * LANES, h * LANES : (h + 1) * LANES]
-                if (k < 4) == in_same:
-                    at = t * OBS_WIDE + h * LANES
-                    gap = off2[:, at : at + LANES] - off_col[k * LANES : (k + 1) * LANES, :]
-                    w = jnp.where(gap * sign >= 0.0, far, near)
-                else:
-                    w = to_same if in_same else to_other
-                line.append(c * w)
+                line.append(c * jnp.where(gap * sign >= 0.0, far, near))
             pieces.append(jnp.concatenate(line, axis=1))
-        gain = split(jnp.concatenate(pieces, axis=0))
-        raw2[:, t * OBS_WIDE : (t + 1) * OBS_WIDE] = raw + dot3((push_hi[...], push_lo[...]), gain)
-    block_setup(1, raw2[...])
-
-    def tile(t, _):
+        return jnp.concatenate(pieces, axis=0)
+
+    def unlike(cov, weight):
+        return cov * jnp.concatenate([jnp.concatenate([weight] * 4, axis=1)] * 4, axis=0)
+
+    same2 = obs_columns(recv_ref, MSG, STATE_ROWS, 1)
+    other2 = obs_columns(other_ref, OBS_ROWS, 0, 1)
+    same2_parts = split(same2)
+    other2_parts = split(other2)
+    left_same = (first_left_hi[...], first_left_lo[...])
+    cov_same = dot3(left_same, same2_parts)
+    _, scaled, push = stats(
+        obs_columns(other_ref, OBS_ROWS, 0, 0), field(field_ref, 0, 1, 4, 8), field(field_ref, 0, 2, 4, 8)
+    )
+    left_hi[...], left_lo[...] = split(scaled.T)
+    push_hi[...], push_lo[...] = split(push)
+    left_other = (left_hi[...], left_lo[...])
+    cov_other = dot3(left_other, same2_parts)
+    push_all = (
+        jnp.concatenate([first_push_hi[...], push_hi[...]], axis=1),
+        jnp.concatenate([first_push_lo[...], push_lo[...]], axis=1),
+    )
+    gain = split(jnp.concatenate([alike(cov_same, 0), unlike(cov_other, to_same)], axis=0))
+    same2 = same2 + dot3(push_all, gain)
+    cov_same = dot3(left_same, other2_parts)
+    cov_other = dot3(left_other, other2_parts)
+    set_const(0, scaled, (push_hi[...], push_lo[...]))
+    _, scaled, push = stats(same2, field(field_ref, 1, 1, 0, 4), field(field_ref, 1, 2, 0, 4))
+    left2_hi[...], left2_lo[...] = split(scaled.T)
+    push2_hi[...], push2_lo[...] = split(push)
+    for s in range(4):
+        thr[s * LANES : (s + 1) * LANES, :] = columns(off2[:, s * LANES : (s + 1) * LANES] + shift)
+    gain = split(jnp.concatenate([unlike(cov_same, to_other), alike(cov_other, HALF)], axis=0))
+    other2 = other2 + dot3(push_all, gain)
+    _, scaled, push = stats(other2, field(field_ref, 1, 1, 4, 8), field(field_ref, 1, 2, 4, 8))
+    set_const(1, scaled, split(push))
+
+    for t in range(NV_DEV // WIDE):
         at = t * (WIDE // LANES)
         before = split(state_columns(recv_ref, at))
-        raw = new_ref[:, pl.ds(pl.multiple_of(t * WIDE, WIDE), WIDE)]
+        raw = new_ref[:, t * WIDE : (t + 1) * WIDE]
         raw = raw + dot3((const_hi[0], const_lo[0]), before)
         centred = split(raw)
-        cov = dot3((left_hi[0:HALF, :], left_lo[0:HALF, :]), centred)
+        cov = dot3((left2_hi[...], left2_lo[...]), centred)
         gain = same_gain(cov, at, thr, low[...], high[...])
         left = (
-            jnp.concatenate([push_hi[:, 0:HALF], const_hi[1]], axis=1),
-            jnp.concatenate([push_lo[:, 0:HALF], const_lo[1]], axis=1),
+            jnp.concatenate([push2_hi[...], const_hi[1]], axis=1),
+            jnp.concatenate([push2_lo[...], const_lo[1]], axis=1),
         )
         right = tuple(jnp.concatenate([g, c], axis=0) for g, c in zip(gain, centred))
         raw = raw + dot3(left, right)
@@ -340,9 +350,6 @@
                 out_ref[pl.ds((at + h) * 2 + r, NDEV, stride=STATE_ROWS), :] = raw[
                     r * NDEV : (r + 1) * NDEV, h * LANES : (h + 1) * LANES
                 ]
-        return 0
-
-    lax.fori_loop(0, NV_DEV // WIDE, tile, 0, unroll=2)
 
 
 VMEM = pl.BlockSpec(memory_space=pltpu.VMEM)
@@ -399,47 +406,47 @@
 def assimilate_first(me, table, fields, recv):
     return pl.pallas_call(
         first_kernel,
-        out_shape=jax.ShapeDtypeStruct((MEMBERS, NV_DEV), F32),
+        out_shape=(
+            jax.ShapeDtypeStruct((MEMBERS, NV_DEV), F32),
+            jax.ShapeDtypeStruct((HALF, MEMBERS), BF16),
+            jax.ShapeDtypeStruct((HALF, MEMBERS), BF16),
+            jax.ShapeDtypeStruct((MEMBERS, HALF), BF16),
+            jax.ShapeDtypeStruct((MEMBERS, HALF), BF16),
+            jax.ShapeDtypeStruct((LANES, LANES), F32),
+            jax.ShapeDtypeStruct((LANES, LANES), F32),
+        ),
         in_specs=[SMEM] + [VMEM] * 3,
+        out_specs=(VMEM,) * 7,
+        scratch_shapes=[pltpu.VMEM((HALF, LANES), F32)],
+        compiler_params=params(VMEM_MIB),
+        cost_estimate=cost(3 * 2**31, 5 * 2**20),
+        name="first",
+    )(me, table, fields, recv)
+
+
+def assimilate(me, table, fields, recv, other, first):
+    return pl.pallas_call(
+        main_kernel,
+        out_shape=jax.ShapeDtypeStruct((NDEV * STATE_ROWS, LANES), F32),
+        in_specs=[SMEM] + [VMEM] * 11,
         out_specs=VMEM,
         scratch_shapes=[
             pltpu.VMEM((HALF, MEMBERS), BF16),
             pltpu.VMEM((HALF, MEMBERS), BF16),
             pltpu.VMEM((MEMBERS, HALF), BF16),
             pltpu.VMEM((MEMBERS, HALF), BF16),
-            pltpu.VMEM((HALF, LANES), F32),
-            pltpu.VMEM((LANES, LANES), F32),
-            pltpu.VMEM((LANES, LANES), F32),
-        ],
-        compiler_params=params(VMEM_MIB),
-        cost_estimate=cost(3 * 2**31, 5 * 2**20),
-        name="first",
-    )(me, table, fields, recv)
-
-
-def assimilate(me, table, fields, recv, other, new):
-    return pl.pallas_call(
-        main_kernel,
-        out_shape=jax.ShapeDtypeStruct((NDEV * STATE_ROWS, LANES), F32),
-        in_specs=[SMEM] + [VMEM] * 5,
-        out_specs=VMEM,
-        scratch_shapes=[
-            pltpu.VMEM((NOBS, MEMBERS), BF16),
-            pltpu.VMEM((NOBS, MEMBERS), BF16),
-            pltpu.VMEM((MEMBERS, NOBS), BF16),
-            pltpu.VMEM((MEMBERS, NOBS), BF16),
+            pltpu.VMEM((HALF, MEMBERS), BF16),
+            pltpu.VMEM((HALF, MEMBERS), BF16),
+            pltpu.VMEM((MEMBERS, HALF), BF16),
+            pltpu.VMEM((MEMBERS, HALF), BF16),
             pltpu.VMEM((2, MEMBERS, MEMBERS), BF16),
             pltpu.VMEM((2, MEMBERS, MEMBERS), BF16),
             pltpu.VMEM((HALF, LANES), F32),
-            pltpu.VMEM((LANES, LANES), F32),
-            pltpu.VMEM((LANES, LANES), F32),
-            pltpu.VMEM((NOBS, LANES), F32),
-            pltpu.VMEM((MEMBERS, NOBS), F32),
         ],
         compiler_params=params(VMEM_MIB),
         cost_estimate=cost(9 * 2**31, 9 * 2**20),
         name="assimilate",
-    )(me, table, fields, recv, other, new)
+    )(me, table, fields, recv, other, *first)
 
 
 def body(prior_state, obs_value, obs_error, obs_owner, obs_offset, taper_table):
@@ -452,8 +459,8 @@
     mine, fields = sort_out(me, obs_owner, obs_offset, obs_value, obs_error, rank, recv)
     other = lax.ppermute(mine, axes, [(i, i ^ 1) for i in range(NDEV)]).reshape(NDEV * OBS_ROWS, LANES)
     recv = recv.reshape(NDEV * MSG, LANES)
-    new = assimilate_first(me, table, fields, recv)
-    new = assimilate(me, table, fields, recv, other, new)
+    first = assimilate_first(me, table, fields, recv)
+    new = assimilate(me, table, fields, recv, other, first)
     back = lax.all_to_all(
         new.reshape(NDEV, STATE_ROWS, LANES), axes, split_axis=0, concat_axis=0, tiled=True
     )

time: 109 us -> 109 us (level)
  no operation moved by 1% of the time
where the time goes in v4:
time: 109 us
  blocking collectives  86.3 us (79%)
  Pallas kernels  19.4 us (18%)
  starting transfers between devices  1.42 us (1%)
  local copies, waits for them, and re-layouts  1.35 us (1%)
    all_to_all x1, blocking collectives, body(): recv = lax.all_to_all(msg, axes, split_axis=0, concat_axis=0, tiled=True)  52.8 us
    all_to_all x1, blocking collectives, body(): lax.all_to_all(new.reshape(NDEV, STATE_ROWS, LANES), axes, split_axis=0,...  33.5 us
    pallas_call x1, Pallas kernels, assimilate(): pl.pallas_call(main_kernel, out_shape=jax.ShapeDtypeStruct((NDEV * STATE_...  12 us
    pallas_call x1, Pallas kernels, assimilate_first(): pl.pallas_call(first_kernel, out_shape=(jax.ShapeDtypeStruct((MEMBERS, NV...  4.32 us
    pallas_call x1, Pallas kernels, prep(): pl.pallas_call(prep_kernel, out_shape=(jax.ShapeDtypeStruct((NDEV, MSG, L...  2.67 us
  transfers between devices with their start and end apart: 1, of which 0 were waited for; matrix products, arithmetic and copies ran while one was open for 0% of the time, Pallas kernels for 4%

profile of v4, /device:TPU:1, one launch (start us, length us, event | category | flops | bytes accessed | tf_op | source)
XLA Modules:
  0.0 108.6 jit_solution(16954441987297777586)
XLA Ops:
  0.0 2.7 %prep.1 = (f32[128,48,128]{2,1,0:T(8,128)S(1)}, f32[2,1024]{1,0:T(2,128)S(1)}) custom-call(s32[1]{0:T(128)} %bitcast.me_ref, s32[2,1024]{1,0:T(2,128)} %owner_ref.1, s32[2,1024]{1,0:T(2,128)} %offset_ref.1, f32[128,32,128]{2,1,0:T(8,128)} %bitcast.21), custom_call_target="tpu_custom_call" | custom-call | tf_op jit(solution)/shard_map/prep/pallas_call | solution.py:373
  2.7 0.0 copy-start
  2.7 0.0 copy-start.1
  2.7 0.0 copy-start.2
  2.7 0.0 copy-start.3
  2.7 52.8 %all_to_all.10.recv_ref = f32[128,48,128]{2,1,0:T(8,128)S(1)} all-to-all(f32[128,48,128]{2,1,0:T(8,128)S(1)} %get-tuple-element.17), channel_id=1, replica_groups=mesh['mem'=4,'var'=32] {'mem','var'}, dimensions={0} | all-to-all | bytes 6291456 | tf_op jit(solution)/shard_map/all_to_all | solution.py:457
  55.6 0.0 copy-start.4
  55.6 0.0 copy-done
  55.6 0.0 copy-done.1
  55.6 0.0 copy-done.2
  55.6 0.0 copy-done.3
  55.6 0.5 fields.1
  56.1 1.4 %collective-permute-start = (f32[128,16,128]{2,1,0:T(8,128)S(1)}, f32[128,16,128]{2,1,0:T(8,128)S(1)}, u32[]{:S(2)}, u32[]{:S(2)}) collective-permute-start(f32[128,16,128]{2,1,0:T(8,128)S(1)} %get-tuple-element.19), channel_id=1, source_target_pairs={{0,1},{1,0},{2,3},{3,2},{4,5},{5,4},{6,7},{7,6},{8,9},{9,8},{10,11... | collective-permute-start | bytes 3145736 | tf_op jit(solution)/shard_map/ppermute | solution.py:460
  57.5 0.0 copy-done.4
  57.5 4.3 %first.1 = (f32[256,2048]{1,0:T(8,128)S(1)}, bf16[512,256]{1,0:T(8,128)(2,1)S(1)}, bf16[512,256]{1,0:T(8,128)(2,1)S(1)}, bf16[256,512]{1,0:T(8,128)(2,1)S(1)}, b...) custom-call(s32[1]{0:T(128)} %bitcast.me_ref, ...), custom_call_target="tpu_custom_call" | custom-call | flops 6442450944 | bytes 5242880 | tf_op jit(solution)/shard_map/first/pallas_call | solution.py:407
  61.8 0.0 collective-permute-done
  61.8 12.0 %assimilate.1 = f32[4096,128]{1,0:T(8,128)S(1)} custom-call(s32[1]{0:T(128)} %bitcast.me_ref, f32[1,128]{1,0:T(1,128)S(1)} %pad_bitcast_fusion.table_ref, f32[48,128]{1,0:T(8,128)S(1)} %get-tuple-element.18.field_ref, f32[6144,128]{1,0:T(8,128)S(1)} %bitcast.17, f32[2048,128]{1,0:T(8,128)S(1)} %bitcast.19, f32[256,2048]{1,0:T(8,128)S(1)} %get-tuple-element.20.new_ref, ...), custom_call_target="tpu_custom_call" | custom-call | flops 19327352832 | bytes 9437184 | tf_op jit(solution)/shard_map/assimilate/pallas_call | solution.py:428
  73.8 33.5 %all_to_all.11 = f32[128,32,128]{2,1,0:T(8,128)S(1)} all-to-all(f32[128,32,128]{2,1,0:T(8,128)S(1)} %bitcast.18), channel_id=1, replica_groups=mesh['mem'=4,'var'=32] {'mem','var'}, dimensions={0} | all-to-all | bytes 4194304 | tf_op jit(solution)/shard_map/all_to_all | solution.py:464
  107.3 1.3 %copy.9 = f32[2,262144]{1,0:T(2,128)} copy(f32[2,262144]{1,0:T(2,128)S(1)} %bitcast.20) | data formatting | bytes 4194304
  (1 shorter events, 0.0 us)
Async XLA Ops:
  2.7 52.9 %copy-start = (s32[2,1024]{1,0:T(2,128)S(1)}, s32[2,1024]{1,0:T(2,128)}, u32[]{:S(2)}) copy-start(s32[2,1024]{1,0:T(2,128)} %owner_ref.1) | copy-start | bytes 24580
  2.7 52.9 %copy-start.1 = (s32[2,1024]{1,0:T(2,128)S(1)}, s32[2,1024]{1,0:T(2,128)}, u32[]{:S(2)}) copy-start(s32[2,1024]{1,0:T(2,128)} %offset_ref.1) | copy-start | bytes 24580
  2.7 52.9 %copy-start.2 = (f32[2,1024]{1,0:T(2,128)S(1)}, f32[2,1024]{1,0:T(2,128)}, u32[]{:S(2)}) copy-start(f32[2,1024]{1,0:T(2,128)} %value_ref.1) | copy-start | bytes 24580
  2.7 52.9 %copy-start.3 = (f32[2,1024]{1,0:T(2,128)S(1)}, f32[2,1024]{1,0:T(2,128)}, u32[]{:S(2)}) copy-start(f32[2,1024]{1,0:T(2,128)} %error_ref.1) | copy-start | bytes 24580
  55.6 1.9 %copy-start.4 = (f32[64]{0:T(128)S(1)}, f32[64]{0:T(128)}, u32[]{:S(2)}) copy-start(f32[64]{0:T(128)} %param.11) | copy-start | bytes 772
  56.1 5.8 %collective-permute-start = (f32[128,16,128]{2,1,0:T(8,128)S(1)}, f32[128,16,128]{2,1,0:T(8,128)S(1)}, u32[]{:S(2)}, u32[]{:S(2)}) collective-permute-start(f32[128,16,128]{2,1,0:T(8,128)S(1)} %get-tuple-element.19), channel_id=1, source_target_pairs={{0,1},{1,0},{2,3},{3,2},{4,5},{5,4},{6,7},{7,6},{8,9},{9,8},{10,11... | collective-permute-start | bytes 3145736 | tf_op jit(solution)/shard_map/ppermute | solution.py:460

commit v5 on v4

--- a/solution.py
+++ b/solution.py
@@ -98,14 +98,18 @@
         rank_ref[b : b + 1, :] = rank
         here = rank == slot
         off = offset_ref[b : b + 1, :]
-        parts = [(off // LANES).astype(F32), (off % LANES).astype(F32)]
-        rows = jnp.concatenate([jnp.where(here, p, 0.0).astype(BF16) for p in parts], axis=0)
+        gap = [jnp.zeros((8, NOBS), F32)]
+        tile_rows = jnp.where(here, (off // LANES).astype(F32), 0.0)
+        lane_rows = jnp.where(here, (off % LANES).astype(F32), 0.0)
+        rows = gap * b + [tile_rows] + gap * 7 + [lane_rows] + gap * (7 - b)
         tables.append(
-            lax.dot_general(rows, hot, (((1,), (1,)), ((), ())), preferred_element_type=F32)
+            lax.dot_general(
+                hot, jnp.concatenate(rows, axis=0).astype(BF16), BOTH_LANES, preferred_element_type=F32
+            )
         )
-    pad = jnp.zeros((LANES - 16, LANES), F32)
-    tile_of = jnp.concatenate([tables[0][0:8], tables[1][0:8], pad], axis=0).T.astype(jnp.int32)
-    lane_of = jnp.concatenate([tables[0][8:16], tables[1][8:16], pad], axis=0).T.astype(jnp.int32)
+    place = tables[0] + tables[1]
+    tile_of = place.astype(jnp.int32)
+    lane_of = pltpu.roll(place, 64, 1).astype(jnp.int32)
     groups = [[], []]
     for g in range(NDEV // 8):
         if g % (share // 8) == 0:

time: 109 us -> 109 us (level)
  no operation moved by 1% of the time
where the time goes in v5:
time: 109 us
  blocking collectives  86.3 us (79%)
  Pallas kernels  19.4 us (18%)
  starting transfers between devices  1.43 us (1%)
  local copies, waits for them, and re-layouts  1.35 us (1%)
    all_to_all x1, blocking collectives, body(): recv = lax.all_to_all(msg, axes, split_axis=0, concat_axis=0, tiled=True)  52.8 us
    all_to_all x1, blocking collectives, body(): lax.all_to_all(new.reshape(NDEV, STATE_ROWS, LANES), axes, split_axis=0,...  33.5 us
    pallas_call x1, Pallas kernels, assimilate(): pl.pallas_call(main_kernel, out_shape=jax.ShapeDtypeStruct((NDEV * STATE_...  12 us
    pallas_call x1, Pallas kernels, assimilate_first(): pl.pallas_call(first_kernel, out_shape=(jax.ShapeDtypeStruct((MEMBERS, NV...  4.33 us
    pallas_call x1, Pallas kernels, prep(): pl.pallas_call(prep_kernel, out_shape=(jax.ShapeDtypeStruct((NDEV, MSG, L...  2.67 us
  transfers between devices with their start and end apart: 1, of which 0 were waited for; matrix products, arithmetic and copies ran while one was open for 0% of the time, Pallas kernels for 4%

profile of v5, /device:TPU:1, one launch (start us, length us, event | category | flops | bytes accessed | tf_op | source)
XLA Modules:
  0.0 108.6 jit_solution(2260633472973844531)
XLA Ops:
  0.0 2.7 %prep.1 = (f32[128,48,128]{2,1,0:T(8,128)S(1)}, f32[2,1024]{1,0:T(2,128)S(1)}) custom-call(s32[1]{0:T(128)} %bitcast.me_ref, s32[2,1024]{1,0:T(2,128)} %owner_ref.1, s32[2,1024]{1,0:T(2,128)} %offset_ref.1, f32[128,32,128]{2,1,0:T(8,128)} %bitcast.21), custom_call_target="tpu_custom_call" | custom-call | tf_op jit(solution)/shard_map/prep/pallas_call | solution.py:377
  2.7 0.0 copy-start
  2.7 0.0 copy-start.1
  2.7 0.0 copy-start.2
  2.7 0.0 copy-start.3
  2.7 52.8 %all_to_all.10.recv_ref = f32[128,48,128]{2,1,0:T(8,128)S(1)} all-to-all(f32[128,48,128]{2,1,0:T(8,128)S(1)} %get-tuple-element.17), channel_id=1, replica_groups=mesh['mem'=4,'var'=32] {'mem','var'}, dimensions={0} | all-to-all | bytes 6291456 | tf_op jit(solution)/shard_map/all_to_all | solution.py:461
  55.6 0.0 copy-start.4
  55.6 0.0 copy-done
  55.6 0.0 copy-done.1
  55.6 0.0 copy-done.2
  55.6 0.0 copy-done.3
  55.6 0.5 fields.1
  56.1 1.4 %collective-permute-start = (f32[128,16,128]{2,1,0:T(8,128)S(1)}, f32[128,16,128]{2,1,0:T(8,128)S(1)}, u32[]{:S(2)}, u32[]{:S(2)}) collective-permute-start(f32[128,16,128]{2,1,0:T(8,128)S(1)} %get-tuple-element.19), channel_id=1, source_target_pairs={{0,1},{1,0},{2,3},{3,2},{4,5},{5,4},{6,7},{7,6},{8,9},{9,8},{10,11... | collective-permute-start | bytes 3145736 | tf_op jit(solution)/shard_map/ppermute | solution.py:464
  57.5 0.0 copy-done.4
  57.5 4.3 %first.1 = (f32[256,2048]{1,0:T(8,128)S(1)}, bf16[512,256]{1,0:T(8,128)(2,1)S(1)}, bf16[512,256]{1,0:T(8,128)(2,1)S(1)}, bf16[256,512]{1,0:T(8,128)(2,1)S(1)}, b...) custom-call(s32[1]{0:T(128)} %bitcast.me_ref, ...), custom_call_target="tpu_custom_call" | custom-call | flops 6442450944 | bytes 5242880 | tf_op jit(solution)/shard_map/first/pallas_call | solution.py:411
  61.8 0.0 collective-permute-done
  61.8 12.0 %assimilate.1 = f32[4096,128]{1,0:T(8,128)S(1)} custom-call(s32[1]{0:T(128)} %bitcast.me_ref, f32[1,128]{1,0:T(1,128)S(1)} %pad_bitcast_fusion.table_ref, f32[48,128]{1,0:T(8,128)S(1)} %get-tuple-element.18.field_ref, f32[6144,128]{1,0:T(8,128)S(1)} %bitcast.17, f32[2048,128]{1,0:T(8,128)S(1)} %bitcast.19, f32[256,2048]{1,0:T(8,128)S(1)} %get-tuple-element.20.new_ref, ...), custom_call_target="tpu_custom_call" | custom-call | flops 19327352832 | bytes 9437184 | tf_op jit(solution)/shard_map/assimilate/pallas_call | solution.py:432
  73.8 33.5 %all_to_all.11 = f32[128,32,128]{2,1,0:T(8,128)S(1)} all-to-all(f32[128,32,128]{2,1,0:T(8,128)S(1)} %bitcast.18), channel_id=1, replica_groups=mesh['mem'=4,'var'=32] {'mem','var'}, dimensions={0} | all-to-all | bytes 4194304 | tf_op jit(solution)/shard_map/all_to_all | solution.py:468
  107.3 1.3 %copy.9 = f32[2,262144]{1,0:T(2,128)} copy(f32[2,262144]{1,0:T(2,128)S(1)} %bitcast.20) | data formatting | bytes 4194304
  (1 shorter events, 0.0 us)
Async XLA Ops:
  2.7 52.9 %copy-start = (s32[2,1024]{1,0:T(2,128)S(1)}, s32[2,1024]{1,0:T(2,128)}, u32[]{:S(2)}) copy-start(s32[2,1024]{1,0:T(2,128)} %owner_ref.1) | copy-start | bytes 24580
  2.7 52.9 %copy-start.1 = (s32[2,1024]{1,0:T(2,128)S(1)}, s32[2,1024]{1,0:T(2,128)}, u32[]{:S(2)}) copy-start(s32[2,1024]{1,0:T(2,128)} %offset_ref.1) | copy-start | bytes 24580
  2.7 52.9 %copy-start.2 = (f32[2,1024]{1,0:T(2,128)S(1)}, f32[2,1024]{1,0:T(2,128)}, u32[]{:S(2)}) copy-start(f32[2,1024]{1,0:T(2,128)} %value_ref.1) | copy-start | bytes 24580
  2.7 52.9 %copy-start.3 = (f32[2,1024]{1,0:T(2,128)S(1)}, f32[2,1024]{1,0:T(2,128)}, u32[]{:S(2)}) copy-start(f32[2,1024]{1,0:T(2,128)} %error_ref.1) | copy-start | bytes 24580
  55.6 1.9 %copy-start.4 = (f32[64]{0:T(128)S(1)}, f32[64]{0:T(128)}, u32[]{:S(2)}) copy-start(f32[64]{0:T(128)} %param.11) | copy-start | bytes 772
  56.1 5.8 %collective-permute-start = (f32[128,16,128]{2,1,0:T(8,128)S(1)}, f32[128,16,128]{2,1,0:T(8,128)S(1)}, u32[]{:S(2)}, u32[]{:S(2)}) collective-permute-start(f32[128,16,128]{2,1,0:T(8,128)S(1)} %get-tuple-element.19), channel_id=1, source_target_pairs={{0,1},{1,0},{2,3},{3,2},{4,5},{5,4},{6,7},{7,6},{8,9},{9,8},{10,11... | collective-permute-start | bytes 3145736 | tf_op jit(solution)/shard_map/ppermute | solution.py:464

commit v6 on v5

--- a/solution.py
+++ b/solution.py
@@ -19,7 +19,7 @@
 OBS_ROWS = 16
 MSG = STATE_ROWS + OBS_ROWS
 PIECES = 1
-WIDE = 1024
+WIDE = 2048
 F32 = jnp.float32
 BF16 = jnp.bfloat16
 VMEM_MIB = 32

time: 109 us -> 109 us (level)
  no operation moved by 1% of the time
where the time goes in v6:
time: 109 us
  blocking collectives  86.3 us (79%)
  Pallas kernels  19.5 us (18%)
  starting transfers between devices  1.43 us (1%)
  local copies, waits for them, and re-layouts  1.35 us (1%)
    all_to_all x1, blocking collectives, body(): recv = lax.all_to_all(msg, axes, split_axis=0, concat_axis=0, tiled=True)  52.8 us
    all_to_all x1, blocking collectives, body(): lax.all_to_all(new.reshape(NDEV, STATE_ROWS, LANES), axes, split_axis=0,...  33.5 us
    pallas_call x1, Pallas kernels, assimilate(): pl.pallas_call(main_kernel, out_shape=jax.ShapeDtypeStruct((NDEV * STATE_...  11.9 us
    pallas_call x1, Pallas kernels, assimilate_first(): pl.pallas_call(first_kernel, out_shape=(jax.ShapeDtypeStruct((MEMBERS, NV...  4.45 us
    pallas_call x1, Pallas kernels, prep(): pl.pallas_call(prep_kernel, out_shape=(jax.ShapeDtypeStruct((NDEV, MSG, L...  2.67 us
  transfers between devices with their start and end apart: 1, of which 0 were waited for; matrix products, arithmetic and copies ran while one was open for 0% of the time, Pallas kernels for 4%

profile of v6, /device:TPU:1, one launch (start us, length us, event | category | flops | bytes accessed | tf_op | source)
XLA Modules:
  0.0 108.7 jit_solution(14231704939529131392)
XLA Ops:
  0.0 2.7 %prep.1 = (f32[128,48,128]{2,1,0:T(8,128)S(1)}, f32[2,1024]{1,0:T(2,128)S(1)}) custom-call(s32[1]{0:T(128)} %bitcast.me_ref, s32[2,1024]{1,0:T(2,128)} %owner_ref.1, s32[2,1024]{1,0:T(2,128)} %offset_ref.1, f32[128,32,128]{2,1,0:T(8,128)} %bitcast.21), custom_call_target="tpu_custom_call" | custom-call | tf_op jit(solution)/shard_map/prep/pallas_call | solution.py:377
  2.7 0.0 copy-start
  2.7 0.0 copy-start.1
  2.7 0.0 copy-start.2
  2.7 0.0 copy-start.3
  2.7 52.8 %all_to_all.10.recv_ref = f32[128,48,128]{2,1,0:T(8,128)S(1)} all-to-all(f32[128,48,128]{2,1,0:T(8,128)S(1)} %get-tuple-element.17), channel_id=1, replica_groups=mesh['mem'=4,'var'=32] {'mem','var'}, dimensions={0} | all-to-all | bytes 6291456 | tf_op jit(solution)/shard_map/all_to_all | solution.py:461
  55.6 0.0 copy-start.4
  55.6 0.0 copy-done
  55.6 0.0 copy-done.1
  55.6 0.0 copy-done.2
  55.6 0.0 copy-done.3
  55.6 0.5 fields.1
  56.1 1.4 %collective-permute-start = (f32[128,16,128]{2,1,0:T(8,128)S(1)}, f32[128,16,128]{2,1,0:T(8,128)S(1)}, u32[]{:S(2)}, u32[]{:S(2)}) collective-permute-start(f32[128,16,128]{2,1,0:T(8,128)S(1)} %get-tuple-element.19), channel_id=1, source_target_pairs={{0,1},{1,0},{2,3},{3,2},{4,5},{5,4},{6,7},{7,6},{8,9},{9,8},{10,11... | collective-permute-start | bytes 3145736 | tf_op jit(solution)/shard_map/ppermute | solution.py:464
  57.5 0.0 copy-done.4
  57.5 4.4 %first.1 = (f32[256,2048]{1,0:T(8,128)S(1)}, bf16[512,256]{1,0:T(8,128)(2,1)S(1)}, bf16[512,256]{1,0:T(8,128)(2,1)S(1)}, bf16[256,512]{1,0:T(8,128)(2,1)S(1)}, b...) custom-call(s32[1]{0:T(128)} %bitcast.me_ref, ...), custom_call_target="tpu_custom_call" | custom-call | flops 6442450944 | bytes 5242880 | tf_op jit(solution)/shard_map/first/pallas_call | solution.py:411
  61.9 0.0 collective-permute-done
  62.0 11.9 %assimilate.1 = f32[4096,128]{1,0:T(8,128)S(1)} custom-call(s32[1]{0:T(128)} %bitcast.me_ref, f32[1,128]{1,0:T(1,128)S(1)} %pad_bitcast_fusion.table_ref, f32[48,128]{1,0:T(8,128)S(1)} %get-tuple-element.18.field_ref, f32[6144,128]{1,0:T(8,128)S(1)} %bitcast.17, f32[2048,128]{1,0:T(8,128)S(1)} %bitcast.19, f32[256,2048]{1,0:T(8,128)S(1)} %get-tuple-element.20.new_ref, ...), custom_call_target="tpu_custom_call" | custom-call | flops 19327352832 | bytes 9437184 | tf_op jit(solution)/shard_map/assimilate/pallas_call | solution.py:432
  73.9 33.5 %all_to_all.11 = f32[128,32,128]{2,1,0:T(8,128)S(1)} all-to-all(f32[128,32,128]{2,1,0:T(8,128)S(1)} %bitcast.18), channel_id=1, replica_groups=mesh['mem'=4,'var'=32] {'mem','var'}, dimensions={0} | all-to-all | bytes 4194304 | tf_op jit(solution)/shard_map/all_to_all | solution.py:468
  107.4 1.3 %copy.9 = f32[2,262144]{1,0:T(2,128)} copy(f32[2,262144]{1,0:T(2,128)S(1)} %bitcast.20) | data formatting | bytes 4194304
  (1 shorter events, 0.0 us)
Async XLA Ops:
  2.7 52.9 %copy-start = (s32[2,1024]{1,0:T(2,128)S(1)}, s32[2,1024]{1,0:T(2,128)}, u32[]{:S(2)}) copy-start(s32[2,1024]{1,0:T(2,128)} %owner_ref.1) | copy-start | bytes 24580
  2.7 52.9 %copy-start.1 = (s32[2,1024]{1,0:T(2,128)S(1)}, s32[2,1024]{1,0:T(2,128)}, u32[]{:S(2)}) copy-start(s32[2,1024]{1,0:T(2,128)} %offset_ref.1) | copy-start | bytes 24580
  2.7 52.9 %copy-start.2 = (f32[2,1024]{1,0:T(2,128)S(1)}, f32[2,1024]{1,0:T(2,128)}, u32[]{:S(2)}) copy-start(f32[2,1024]{1,0:T(2,128)} %value_ref.1) | copy-start | bytes 24580
  2.7 52.9 %copy-start.3 = (f32[2,1024]{1,0:T(2,128)S(1)}, f32[2,1024]{1,0:T(2,128)}, u32[]{:S(2)}) copy-start(f32[2,1024]{1,0:T(2,128)} %error_ref.1) | copy-start | bytes 24580
  55.6 1.9 %copy-start.4 = (f32[64]{0:T(128)S(1)}, f32[64]{0:T(128)}, u32[]{:S(2)}) copy-start(f32[64]{0:T(128)} %param.11) | copy-start | bytes 772
  56.1 5.9 %collective-permute-start = (f32[128,16,128]{2,1,0:T(8,128)S(1)}, f32[128,16,128]{2,1,0:T(8,128)S(1)}, u32[]{:S(2)}, u32[]{:S(2)}) collective-permute-start(f32[128,16,128]{2,1,0:T(8,128)S(1)} %get-tuple-element.19), channel_id=1, source_target_pairs={{0,1},{1,0},{2,3},{3,2},{4,5},{5,4},{6,7},{7,6},{8,9},{9,8},{10,11... | collective-permute-start | bytes 3145736 | tf_op jit(solution)/shard_map/ppermute | solution.py:464
